TPU v7x, 32 devices: a whole 2x2x4 slice. The times are simulated.
32 devices in a mesh: blk: 4 (over y, x), seg: 8 (over z, core).
Axes of the slice: x: 2, y: 2, z: 4, core: 2. Of those that a mesh axis runs over, the one named last changes fastest.
Arguments:
- spectra: bfloat16 [8, 512, 2, 4096], P(None, ('blk', 'seg')), may hold values from -6 to 6
- fibre_lists: int32 [8, 64], replicated, may hold values from 0 to 511, as said below
- pairing: int32 [1, 8], replicated, may hold values from 0 to 7, as said below
Outputs:
- stack: float32 [1, 8, 64, 64, 128], P(None, 'blk', 'seg')
Inputs may be any that keep to these rules, and one draw needn't show every extreme that they name: `fibre_lists`: row b lists the 64 channels of block b in an arbitrary order; every channel number appears exactly once in the table. Within every aligned range of 128 consecutive channel numbers, no block has more than 24 of its channels, and some block has exactly 24. `pairing`: row r maps every block to its partner in round r: the partner of the partner is the block itself, no block is its own partner, and no two rounds pair the same two blocks.
All inputs are finite; a program needn't handle non-finite values.
Results may differ from a plain program's by a relative error of at most 0.0037.
Values may be sent and summed in bfloat16 or wider, within the bound.
A program may use at most 192 MiB of HBM per device.

v0:
```python
import math

import jax
import jax.numpy as jnp
from jax import lax
from jax.sharding import PartitionSpec as P

LH = 128


def make_table(frequencies, lag_count):
    freq_ids = jnp.arange(frequencies, dtype=jnp.int32)[:, None]
    lag_ids = jnp.arange(lag_count, dtype=jnp.int32)[None, :]
    angles = (freq_ids * lag_ids % (2 * frequencies)).astype(jnp.float32) * (math.pi / frequencies)
    return jnp.concatenate([jnp.cos(angles), -jnp.sin(angles)], 0).astype(jnp.bfloat16)


def cross_lags(left_rows, right_rows, lag_table):
    left_re = left_rows[:, 0].astype(jnp.float32)
    left_im = left_rows[:, 1].astype(jnp.float32)
    right_re = right_rows[:, 0].astype(jnp.float32)
    right_im = right_rows[:, 1].astype(jnp.float32)
    real_part = left_re[:, None, :] * right_re[None] + left_im[:, None, :] * right_im[None]
    imag_part = left_im[:, None, :] * right_re[None] - left_re[:, None, :] * right_im[None]
    spectrum = jnp.concatenate([real_part, imag_part], -1).astype(jnp.bfloat16)
    spectrum = spectrum.reshape(-1, spectrum.shape[-1])
    product = jnp.dot(spectrum, lag_table, preferred_element_type=jnp.float32)
    return product.reshape(left_rows.shape[0], right_rows.shape[0], -1)


def pair_terms(own_panels, others, lag_table, row_count):
    seg_local = own_panels.shape[0]
    blk_local = own_panels.shape[1]
    units = others.shape[1]
    channels = others.shape[2]
    lag_count = lag_table.shape[1]
    sub_rows = math.gcd(row_count, max(1, 512 // channels))

    def unit_term(unit_index):
        left_all = lax.dynamic_index_in_dim(own_panels, unit_index % blk_local, 1, keepdims=False)
        right_all = lax.dynamic_index_in_dim(others, unit_index, 1, keepdims=False)

        def accumulate(step, running):
            left_rows = lax.dynamic_index_in_dim(left_all, step, 0, keepdims=False)
            right_rows = lax.dynamic_index_in_dim(right_all, step, 0, keepdims=False)
            pieces = [
                cross_lags(left_rows[offset : offset + sub_rows], right_rows, lag_table)
                for offset in range(0, row_count, sub_rows)
            ]
            return running + jnp.concatenate(pieces, 0)

        return lax.fori_loop(
            0, seg_local, accumulate, jnp.zeros((row_count, channels, lag_count), jnp.float32)
        )

    terms = lax.map(unit_term, jnp.arange(units, dtype=jnp.int32))
    return jnp.moveaxis(terms, 1, 0).reshape(
        row_count, units // blk_local, blk_local, channels, lag_count
    )


def local(spectra, fibre_lists, pairing):
    frequencies = spectra.shape[-1]
    blk_count = lax.axis_size("blk")
    seg_count = lax.axis_size("seg")
    blk_index = lax.axis_index("blk")
    block_count, channels = fibre_lists.shape
    blk_local = block_count // blk_count
    bound_rows = 3 * channels // (2 * blk_count)
    column = lax.all_to_all(spectra, "seg", split_axis=0, concat_axis=1, tiled=True)
    seg_local = column.shape[0]
    width = column.shape[1]
    mine_ids = blk_index * blk_local + jnp.arange(blk_local, dtype=jnp.int32)
    partners = jnp.take(pairing, mine_ids, axis=1).reshape(-1)
    local_rows = fibre_lists - blk_index * width
    inside = (local_rows >= 0) & (local_rows < width)
    outgoing = jnp.sort(jnp.where(inside, local_rows, width), axis=1)[:, :bound_rows]
    packed = jnp.take(column, outgoing.reshape(-1), axis=1, mode="fill", fill_value=0)
    packed = packed.reshape(seg_local, blk_count, blk_local * bound_rows, 2, frequencies)
    arrived = lax.all_to_all(packed, "blk", split_axis=1, concat_axis=1, tiled=True)
    arrived = arrived.reshape(seg_local, blk_count * blk_local * bound_rows, 2, frequencies)
    wanted = jnp.take(fibre_lists, mine_ids, axis=0)
    source = wanted // width
    same_column = (source[:, :, None] == source[:, None, :]) & (
        wanted[:, None, :] < wanted[:, :, None]
    )
    rank_within = jnp.sum(same_column.astype(jnp.int32), axis=2)
    slot_index = (
        source * (blk_local * bound_rows)
        + jnp.arange(blk_local, dtype=jnp.int32)[:, None] * bound_rows
        + rank_within
    )
    own_panels = jnp.take(arrived, slot_index.reshape(-1), axis=1).reshape(
        seg_local, blk_local, channels, 2, frequencies
    )
    panels = lax.all_gather(own_panels, "blk", axis=1, tiled=True)
    others = jnp.take(panels, partners, axis=1)
    lag_table = make_table(frequencies, LH)
    share_rows = channels // seg_count
    scaling = 1.0 / math.sqrt(frequencies * seg_local * seg_count)
    summed = lax.psum(pair_terms(own_panels, others, lag_table, channels), "seg")
    kept_rows = lax.dynamic_slice_in_dim(summed, lax.axis_index("seg") * share_rows, share_rows, 0)
    return jnp.transpose(kept_rows, (1, 2, 0, 3, 4)) * scaling


def solution(mesh):
    in_specs = (P(None, ("blk", "seg"), None, None), P(), P())
    out_specs = P(None, "blk", "seg", None, None)
    return jax.shard_map(local, mesh=mesh, in_specs=in_specs, out_specs=out_specs, check_vma=False)
```

profile of v0, /device:TPU:25, one launch (start us, length us, event | category | flops | bytes accessed | tf_op | source)
XLA Modules:
  0.0 472.6 jit_solution(17849602042736874821)
XLA Ops:
  6.5 5.5 %all-to-all-start = ((bf16[8,16,2,4096]{3,2,1,0:T(2,128)(2,1)}), bf16[8,16,2,4096]{3,2,1,0:T(2,128)(2,1)S(1)}, u32[]{:S(2)}, u32[]{:S(2)}) async-start(bf16[8,16,2,4096]{3,2,1,0:T(2,128)(2,1)} %param.5), calls=%async_computation | async-start | bytes 4194304 | tf_op jit(solution)/shard_map/all_to_all | solution.py:70
  12.2 1.0 sort.15
  13.5 45.0 %all-to-all-done = bf16[8,16,2,4096]{3,2,1,0:T(2,128)(2,1)S(1)} async-done(((bf16[8,16,2,4096]{3,2,1,0:T(2,128)(2,1)}), bf16[8,16,2,4096]{3,2,1,0:T(2,128)(2,1)S(1)}, u32[]{:S(2)}, u32[]{:S(2)}) %all-to-all-start) | async-done | bytes 2097184 | tf_op jit(solution)/shard_map/all_to_all | solution.py:70
  58.5 11.0 %gather_fusion.1 = bf16[192,2,4096]{2,1,0:T(2,128)(2,1)} fusion(bf16[128,2,4096]{2,1,0:T(2,128)(2,1)S(1)} %bitcast.207, s32[1024]{0:T(1024)S(1)} %pad_clamp_fusion.2), kind=kCustom, calls=%fused_computation.1 | custom fusion | bytes 6292224 | tf_op jit(solution)/shard_map/jit(_take)/gather | solution.py:78
  69.5 6.3 %broadcast_select_fusion = bf16[1,4,48,2,4096]{4,3,2,0,1:T(2,128)(2,1)} fusion(bf16[1,4,48,2,4096]{4,3,2,0,1:T(2,128)(2,1)} %bitcast.208, pred[4,48]{1,0:T(4,128)(4,1)S(1)} %compare_and_fusion.1), kind=kLoop, calls=%fused_computation.124 | loop fusion | flops 1572864 | bytes 6291648 | tf_op jit(solution)/shard_map/jit(_take)/select_n | solution.py:78
  75.8 3.7 all-to-all-start.1
  81.1 34.1 %all-to-all-done.1 = bf16[1,4,48,2,4096]{4,3,2,0,1:T(2,128)(2,1)S(1)} async-done(((bf16[1,4,48,2,4096]{4,3,2,0,1:T(2,128)(2,1)}), bf16[1,4,48,2,4096]{4,3,2,0,1:T(2,128)(2,1)S(1)}, u32[]{:S(2)}, u32[]{:S(2)}) %all-to-all-start.1) | async-done | bytes 3145760 | tf_op jit(solution)/shard_map/all_to_all | solution.py:80
  115.2 8.0 %gather_fusion.2 = bf16[128,2,4096]{2,1,0:T(2,128)(2,1)} fusion(bf16[192,2,4096]{2,1,0:T(2,128)(2,1)S(1)} %bitcast.209, s32[1024]{0:T(1024)S(1)} %pad_clamp_fusion.1), kind=kCustom, calls=%fused_computation.2 | custom fusion | bytes 4194816 | tf_op jit(solution)/shard_map/jit(_take)/gather | solution.py:93
  123.1 2.9 copy.22
  126.1 1.7 broadcast_select_fusion.1
  127.8 0.6 gather_fusion.3
  128.5 8.6 %negate_convert_fusion = (bf16[4096,128]{1,0:T(8,128)(2,1)S(1)}, bf16[4096,128]{1,0:T(8,128)(2,1)S(1)}) fusion(), kind=kLoop, calls=%fused_computation.133 | loop fusion | flops 8912896 | bytes 2097152 | tf_op jit(solution)/shard_map/convert.35
  137.1 1.5 pad_maximum_fusion
  138.6 77.6 %all-gather.2.cloned.1.call-done = bf16[1,8,64,2,4096]{4,2,1,3,0:T(8,128)(2,1)} async-done(((bf16[1,2,64,2,4096]{4,2,1,3,0:T(8,128)(2,1)}), bf16[1,8,64,2,4096]{4,2,1,3,0:T(8,128)(2,1)}) %all-gather.2.cloned.1.call-update) | async-done | bytes 8388624 | tf_op jit(solution)/shard_map/all_gather | solution.py:96
  216.2 5.5 %gather_fusion.4 = bf16[2,64,2,4096]{3,1,2,0:T(8,128)(2,1)} fusion(bf16[8,64,2,4096]{3,1,0,2:T(8,128)(2,1)} %bitcast.211, s32[1024]{0:T(1024)S(1)} %pad_clamp_fusion), kind=kCustom, calls=%fused_computation.4 | custom fusion | bytes 4194312 | tf_op jit(solution)/shard_map/jit(_take)/gather | solution.py:97
  221.7 3.2 bitcast_select_fusion
  224.9 143.0 %while.13 = (s32[]{:T(128)}, f32[2,64,64,128]{3,2,1,0:T(8,128)}, s32[2]{0:T(128)S(1)}, bf16[1,2,64,2,4096]{4,2,1,3,0:T(8,128)(2,1)S(1)}, bf16[1,2,64,2,4096]{4,2...) while((s32[]{:T(128)}, f32[2,64,64,128]{3,2,1,0:T(8,128)}, ...), condition=%wide.region_3.4_spmd, body=%wide.region_2.3_spmd.sunk | while | flops 8859418624 | bytes 385877280 | solution.py:56
  224.9 0.6 dynamic_slice.37
  227.7 0.7 fusion.164
  228.4 0.8 fusion.160
  230.5 1.4 dynamic-slice_bitcast_fusion.5
  232.1 28.8 %add_convert_fusion.9 = (bf16[8,64,4096]{2,1,0:T(8,128)(2,1)S(1)}, bf16[8,64,4096]{2,1,0:T(8,128)(2,1)S(1)}, bf16[8,64,4096]{2,1,0:T(8,128)(2,1)}, bf16[8,64,409...) fusion(f32[8,4096]{1,0:T(8,128)S(1)} %copy-done.17, ...), kind=kLoop, calls=%fused_computation.38.clone.1 | loop fusion | flops 134217728 | bytes 71303168 | tf_op jit(solution)/shard_map/convert.18
  260.9 5.9 %fusion.165 = f32[64,64,128]{2,1,0:T(8,128)S(1)} fusion(bf16[8192,128]{1,0:T(8,128)(2,1)} %get-tuple-element.353, bf16[8,64,4096]{2,1,0:T(8,128)(2,1)} %get-tuple-element.314, bf16[8,64,4096]{2,1,0:T(8,128)(2,1)} %get-tuple-element.315), kind=kOutput, calls=%fused_computation.69.clone.1 | convolution fusion | flops 1090519040 | bytes 10747904 | tf_op jit(solution)/shard_map/while/body/eval_jaxpr/while/body/eval_jaxpr/dot_general | solution.py:27
  266.8 0.6 copy-done.13
  267.5 4.1 fusion.166
  271.6 4.1 fusion.167
  275.7 4.1 fusion.168
  279.8 4.1 fusion.169
  284.0 4.1 fusion.170
  288.1 4.1 fusion.171
  292.2 2.7 fusion.172
  294.9 1.5 bitcast_dynamic-update-slice_fusion.2
  299.2 0.7 fusion.164
  299.9 0.8 fusion.160
  302.0 1.4 dynamic-slice_bitcast_fusion.5
  303.6 28.8 %add_convert_fusion.9 = (bf16[8,64,4096]{2,1,0:T(8,128)(2,1)S(1)}, bf16[8,64,4096]{2,1,0:T(8,128)(2,1)S(1)}, bf16[8,64,4096]{2,1,0:T(8,128)(2,1)}, bf16[8,64,409...) fusion(f32[8,4096]{1,0:T(8,128)S(1)} %copy-done.17, ...), kind=kLoop, calls=%fused_computation.38.clone.1 | loop fusion | flops 134217728 | bytes 71303168 | tf_op jit(solution)/shard_map/convert.18
  332.4 5.9 %fusion.165 = f32[64,64,128]{2,1,0:T(8,128)S(1)} fusion(bf16[8192,128]{1,0:T(8,128)(2,1)} %get-tuple-element.353, bf16[8,64,4096]{2,1,0:T(8,128)(2,1)} %get-tuple-element.314, bf16[8,64,4096]{2,1,0:T(8,128)(2,1)} %get-tuple-element.315), kind=kOutput, calls=%fused_computation.69.clone.1 | convolution fusion | flops 1090519040 | bytes 10747904 | tf_op jit(solution)/shard_map/while/body/eval_jaxpr/while/body/eval_jaxpr/dot_general | solution.py:27
  338.3 0.6 copy-done.13
  339.0 4.1 fusion.166
  343.1 4.1 fusion.167
  347.2 4.1 fusion.168
  351.3 4.1 fusion.169
  355.5 4.1 fusion.170
  359.6 4.1 fusion.171
  363.7 2.7 fusion.172
  366.4 1.4 bitcast_dynamic-update-slice_fusion.2
  367.9 95.9 %all-reduce.2.cloned.1.call-done = f32[64,1,2,64,128]{4,3,0,2,1:T(8,128)} async-done(((f32[64,1,2,64,128]{4,3,0,2,1:T(8,128)}), f32[64,1,2,64,128]{4,3,0,2,1:T(8,128)}) %all-reduce.2.cloned.1.call-update) | async-done | bytes 4194320 | tf_op jit(solution)/shard_map/psum | solution.py:101
  463.8 1.9 multiply_bitcast_fusion
  (118 shorter events, 3.6 us)
Async XLA Ops:
  6.5 121.3 %copy-start = (s32[1,8]{1,0:T(1,128)S(1)}, s32[1,8]{1,0:T(1,128)}, u32[]{:S(2)}) copy-start(s32[1,8]{1,0:T(1,128)} %param.7) | copy-start | bytes 100
  6.5 5.5 %copy-start.20 = (s32[8,64]{1,0:T(8,128)S(1)}, s32[8,64]{1,0:T(8,128)}, u32[]{:S(2)}) copy-start(s32[8,64]{1,0:T(8,128)} %param.6) | copy-start | bytes 6148
  6.5 52.0 %all-to-all-start = ((bf16[8,16,2,4096]{3,2,1,0:T(2,128)(2,1)}), bf16[8,16,2,4096]{3,2,1,0:T(2,128)(2,1)S(1)}, u32[]{:S(2)}, u32[]{:S(2)}) async-start(bf16[8,16,2,4096]{3,2,1,0:T(2,128)(2,1)} %param.5), calls=%async_computation | async-start | bytes 4194304 | tf_op jit(solution)/shard_map/all_to_all | solution.py:70
  75.8 39.4 %all-to-all-start.1 = ((bf16[1,4,48,2,4096]{4,3,2,0,1:T(2,128)(2,1)}), bf16[1,4,48,2,4096]{4,3,2,0,1:T(2,128)(2,1)S(1)}, u32[]{:S(2)}, u32[]{:S(2)}) async-start(bf16[1,4,48,2,4096]{4,3,2,0,1:T(2,128)(2,1)} %broadcast_select_fusion), calls=%async_computation.1 | async-start | bytes 6291456 | tf_op jit(solution)/shard_map/all_to_all | solution.py:80
  79.5 136.7 %all-gather.2.cloned.1.call-start = ((), (), s32[]{:S(2)}) async-start(), calls=%async_computation.2 | async-start | bytes 10485760 | tf_op jit(solution)/shard_map/all_gather | solution.py:96
  127.7 336.1 %all-reduce.2.cloned.1.call-start = ((), (), s32[]{:S(2)}) async-start(), calls=%async_computation.3 | async-start | bytes 8388608 | tf_op jit(solution)/shard_map/psum | solution.py:101
  216.2 8.7 %copy-start.14 = (bf16[1,2,64,2,4096]{4,2,1,3,0:T(8,128)(2,1)S(1)}, bf16[1,2,64,2,4096]{4,2,1,3,0:T(8,128)(2,1)}, u32[]{:S(2)}) copy-start(bf16[1,2,64,2,4096]{4,2,1,3,0:T(8,128)(2,1)} %broadcast_select_fusion.1) | copy-start | bytes 6291460
  230.5 1.6 copy-start.15
  230.5 1.6 copy-start.16
  230.5 1.6 copy-start.17
  230.5 1.6 copy-start.18
  260.9 5.9 %copy-start.12 = (bf16[8,64,4096]{2,1,0:T(8,128)(2,1)S(1)}, bf16[8,64,4096]{2,1,0:T(8,128)(2,1)}, u32[]{:S(2)}) copy-start(bf16[8,64,4096]{2,1,0:T(8,128)(2,1)} %get-tuple-element.316) | copy-start | bytes 12582916 | tf_op jit(solution)/shard_map/while
  260.9 6.5 %copy-start.13 = (bf16[8,64,4096]{2,1,0:T(8,128)(2,1)S(1)}, bf16[8,64,4096]{2,1,0:T(8,128)(2,1)}, u32[]{:S(2)}) copy-start(bf16[8,64,4096]{2,1,0:T(8,128)(2,1)} %get-tuple-element.317) | copy-start | bytes 12582916 | tf_op jit(solution)/shard_map/while
  267.5 4.1 copy-start.10
  267.5 4.1 copy-start.11
  271.6 4.1 copy-start.8
  271.6 4.1 copy-start.9
  275.7 4.1 copy-start.6
  275.7 4.1 copy-start.7
  279.8 4.1 copy-start.4
  279.8 4.1 copy-start.5
  283.9 4.1 copy-start.2
  283.9 4.1 copy-start.3
  288.1 4.1 copy-start.19
  302.0 1.6 copy-start.15
  302.0 1.6 copy-start.16
  302.0 1.6 copy-start.17
  302.0 1.6 copy-start.18
  332.4 5.9 %copy-start.12 = (bf16[8,64,4096]{2,1,0:T(8,128)(2,1)S(1)}, bf16[8,64,4096]{2,1,0:T(8,128)(2,1)}, u32[]{:S(2)}) copy-start(bf16[8,64,4096]{2,1,0:T(8,128)(2,1)} %get-tuple-element.316) | copy-start | bytes 12582916 | tf_op jit(solution)/shard_map/while
  332.4 6.5 %copy-start.13 = (bf16[8,64,4096]{2,1,0:T(8,128)(2,1)S(1)}, bf16[8,64,4096]{2,1,0:T(8,128)(2,1)}, u32[]{:S(2)}) copy-start(bf16[8,64,4096]{2,1,0:T(8,128)(2,1)} %get-tuple-element.317) | copy-start | bytes 12582916 | tf_op jit(solution)/shard_map/while
  339.0 4.1 copy-start.10
  339.0 4.1 copy-start.11
  343.1 4.1 copy-start.8
  343.1 4.1 copy-start.9
  347.2 4.1 copy-start.6
  347.2 4.1 copy-start.7
  351.3 4.1 copy-start.4
  351.3 4.1 copy-start.5
  355.5 4.1 copy-start.2
  355.5 4.1 copy-start.3
  359.6 4.1 copy-start.19
  367.9 97.8 %copy-start.1 = (s32[1,8]{1,0:T(1,128)S(1)}, s32[1,8]{1,0:T(1,128)}, u32[]{:S(2)}) copy-start(s32[1,8]{1,0:T(1,128)} %param.7) | copy-start | bytes 100
Sparse Core Ops, SparseCore 0:
  127.9 88.2 all-gather.1
  368.0 95.7 all-reduce.1
where the time goes:
time: 476 us; the launch traced here: 473 us
  waiting for transfers between devices  253 us (53%)
  other arithmetic  85.7 us (18%)
  matrix products  66.2 us (14%)
  local copies, waits for them, and re-layouts  37.9 us (8%)
  between operations  13.5 us (3%)
  starting transfers between devices  9.51 us (2%)
  loops' own time  7.09 us (1%)
    psum x1, waiting for transfers between devices, local(): lax.psum(pair_terms(own_panels, others, lag_table, channels), 'seg')  95.9 us
    all_gather x1, waiting for transfers between devices, local(): panels = lax.all_gather(own_panels, 'blk', axis=1, tiled=True)  77.6 us
    another operation x3, other arithmetic  66.2 us
    dot_general x16, matrix products, cross_lags(): product = jnp.dot(spectrum, lag_table, preferred_element_type=jnp.float32)  66.2 us
    all_to_all x1, waiting for transfers between devices, local(): lax.all_to_all(spectra, 'seg', split_axis=0, concat_axis=1, tiled=True)  45 us
    all_to_all x1, waiting for transfers between devices, local(): lax.all_to_all(packed, 'blk', split_axis=1, concat_axis=1, tiled=True)  34.1 us
    gather x1, local copies, waits for them, and re-layouts, local(): jnp.take(column, outgoing.reshape(-1), axis=1, mode='fill', fill_value=0)  11 us
    gather x2, local copies, waits for them, and re-layouts, local(): jnp.take(arrived, slot_index.reshape(-1), axis=1)  10.9 us
  transfers between devices with their start and end apart: 4, of which 4 were waited for; matrix products, arithmetic and copies ran while one was open for 3% of the time, Pallas kernels for 0%

commit v1 on v0

v1 whole, which is shorter than its diff:
```python
import functools
import math

import numpy as np
import jax
import jax.numpy as jnp
from jax import lax
from jax.experimental import pallas as pl
from jax.experimental.pallas import tpu as pltpu
from jax.sharding import PartitionSpec as P

LH = 128
STEP = 16
COARSE = LH // STEP
FINE = STEP // 2
CHUNK = 512
NT = (((1,), (1,)), ((), ()))


def phase_tables(frequencies):
    freq = np.arange(frequencies, dtype=np.float64)[None, :]
    coarse = (STEP * np.arange(COARSE, dtype=np.float64) + (STEP - 1) / 2)[:, None]
    fine = (np.arange(FINE, dtype=np.float64) + 0.5)[:, None]
    angles = np.concatenate([coarse, fine], 0) * freq * (math.pi / frequencies)
    return np.cos(angles).astype(np.float32), np.sin(angles).astype(np.float32)


def take_small(table, index):
    hit = index[:, None] == jnp.arange(table.shape[0], dtype=jnp.int32)[None, :]
    return jnp.sum(jnp.where(hit, table[None, :], 0), axis=1)


def assign(partner):
    count = partner.shape[0]
    blocks = jnp.arange(count, dtype=jnp.int32)
    hop = partner ^ 1
    lowest = blocks
    for _ in range(max(1, (count // 2 - 1).bit_length())):
        lowest = jnp.minimum(lowest, take_small(lowest, hop))
        hop = take_small(hop, hop)
    return lowest < take_small(lowest, blocks ^ 1)


def correlate_kernel(chan, arrived, unpack, cos_ref, sin_ref, plus_ref, minus_ref, xp, xm, yp):
    step = pl.program_id(0)
    width = arrived.shape[1]

    @pl.when(step == 0)
    def _():
        plus_ref[...] = jnp.zeros_like(plus_ref)
        minus_ref[...] = jnp.zeros_like(minus_ref)

    rows = jnp.dot(unpack[...], arrived[...], preferred_element_type=jnp.float32)
    xr, yr = rows[0:chan], rows[chan : 2 * chan]
    xi, yi = rows[2 * chan : 3 * chan], rows[3 * chan : 4 * chan]
    re, im = pl.ds(0, width), pl.ds(width, width)
    bf = jnp.bfloat16
    for a in range(COARSE):
        c, s = cos_ref[a : a + 1, :], sin_ref[a : a + 1, :]
        rc, rs, ic, i_s = xr * c, xr * s, xi * c, xi * s
        at = pl.ds(a * chan, chan)
        xp[at, re] = (rc - i_s).astype(bf)
        xp[at, im] = (ic + rs).astype(bf)
        xm[at, re] = (rc + i_s).astype(bf)
        xm[at, im] = (ic - rs).astype(bf)
    for m in range(FINE):
        c, s = cos_ref[COARSE + m : COARSE + m + 1, :], sin_ref[COARSE + m : COARSE + m + 1, :]
        rc, rs, ic, i_s = yr * c, yr * s, yi * c, yi * s
        at, back = pl.ds((FINE + m) * chan, chan), pl.ds((FINE - 1 - m) * chan, chan)
        yp[at, re] = (rc + i_s).astype(bf)
        yp[at, im] = (ic - rs).astype(bf)
        yp[back, re] = (rc - i_s).astype(bf)
        yp[back, im] = (ic + rs).astype(bf)

    tile = 256

    @pl.loop(0, yp.shape[0] // tile)
    def _(t):
        at = pl.ds(pl.multiple_of(t * tile, tile), tile)
        y = yp[at, :]
        plus_ref[:, at] += lax.dot_general(xp[...], y, NT, preferred_element_type=jnp.float32)
        minus_ref[at, :] += lax.dot_general(y, xm[...], NT, preferred_element_type=jnp.float32)


def correlate(arrived, unpack, chan):
    total, frequencies = arrived.shape
    cos, sin = phase_tables(frequencies)
    wide = COARSE * chan
    return pl.pallas_call(
        functools.partial(correlate_kernel, chan),
        grid=(frequencies // CHUNK,),
        in_specs=[
            pl.BlockSpec((total, CHUNK), lambda k: (0, k)),
            pl.BlockSpec(unpack.shape, lambda k: (0, 0)),
            pl.BlockSpec((COARSE + FINE, CHUNK), lambda k: (0, k)),
            pl.BlockSpec((COARSE + FINE, CHUNK), lambda k: (0, k)),
        ],
        out_specs=[
            pl.BlockSpec((wide, 2 * wide), lambda k: (0, 0)),
            pl.BlockSpec((2 * wide, wide), lambda k: (0, 0)),
        ],
        out_shape=[
            jax.ShapeDtypeStruct((wide, 2 * wide), jnp.float32),
            jax.ShapeDtypeStruct((2 * wide, wide), jnp.float32),
        ],
        scratch_shapes=[
            pltpu.VMEM((wide, 2 * CHUNK), jnp.bfloat16),
            pltpu.VMEM((wide, 2 * CHUNK), jnp.bfloat16),
            pltpu.VMEM((2 * wide, 2 * CHUNK), jnp.bfloat16),
        ],
        compiler_params=pltpu.CompilerParams(
            dimension_semantics=("arbitrary",), vmem_limit_bytes=48 * 1024 * 1024
        ),
        cost_estimate=pl.CostEstimate(
            flops=8 * wide * wide * frequencies * 2,
            bytes_accessed=total * frequencies * 2 + 16 * wide * wide,
            transcendentals=0,
        ),
    )(arrived, unpack, cos, sin)


def local(spectra, fibre_lists, pairing):
    seg_all, held, _, frequencies = spectra.shape
    blk_count = lax.axis_size("blk")
    seg_count = lax.axis_size("seg")
    blk_index = lax.axis_index("blk")
    block_count, chan = fibre_lists.shape
    width = held * seg_count
    bound = 2 * (3 * chan // (2 * blk_count))
    partner = pairing[0]

    blocks = jnp.arange(block_count, dtype=jnp.int32)
    leads = assign(partner)
    owner = jnp.where(leads, blocks, partner) // 2
    lead_parity = (~leads[0::2]).astype(jnp.int32)
    lead = 2 * jnp.arange(blk_count, dtype=jnp.int32) + lead_parity
    follow = take_small(partner, lead)
    i32 = jnp.int32

    mine = blk_index * width + jnp.arange(width, dtype=i32)
    flat = fibre_lists.reshape(-1)
    flat_owner = jnp.repeat(owner, chan)
    pair_of = jnp.sum(jnp.where(flat[:, None] == mine[None, :], flat_owner[:, None], 0), axis=0)
    order = jnp.arange(width, dtype=i32)
    rank = jnp.sum((pair_of[:, None] == pair_of[None, :]) & (order[:, None] < order[None, :]), axis=0).astype(i32)
    spot = pair_of * bound + rank
    hit = jnp.arange(blk_count * bound, dtype=i32)[:, None] == spot[None, :]
    hit = hit.reshape(blk_count, 1, bound, seg_count, 1, held)
    part = jnp.arange(2, dtype=i32)
    same = (part[:, None] == part[None, :]).reshape(1, 2, 1, 1, 2, 1)
    pack = (hit & same).astype(jnp.bfloat16).reshape(blk_count * 2 * bound, 2 * width)

    pair = jnp.concatenate(
        [jnp.take(fibre_lists, lead[blk_index], axis=0), jnp.take(fibre_lists, follow[blk_index], axis=0)]
    )
    source = pair // width
    rank = jnp.sum((source[:, None] == source[None, :]) & (pair[None, :] < pair[:, None]), axis=1).astype(i32)
    spot = source * bound + rank
    hit = spot[:, None] == jnp.arange(blk_count * bound, dtype=i32)[None, :]
    hit = hit.reshape(1, 2 * chan, blk_count, 1, bound)
    same = (part[:, None] == part[None, :]).reshape(2, 1, 1, 2, 1)
    unpack = (hit & same).astype(jnp.bfloat16).reshape(4 * chan, blk_count * 2 * bound)

    rows = jnp.transpose(spectra, (0, 2, 1, 3)).reshape(seg_all, 2 * held, frequencies)
    column = lax.all_to_all(rows, "seg", split_axis=0, concat_axis=0, tiled=True)
    column = column.reshape(seg_count * 2 * held, frequencies)
    packed = jnp.dot(pack, column, preferred_element_type=jnp.float32).astype(jnp.bfloat16)
    packed = packed.reshape(blk_count, 2 * bound, frequencies)
    arrived = lax.all_to_all(packed, "blk", split_axis=0, concat_axis=0, tiled=True)
    plus, minus = correlate(arrived.reshape(blk_count * 2 * bound, frequencies), unpack, chan)

    share = chan // seg_count
    plus = plus.reshape(COARSE, seg_count, share, 2 * FINE * chan)
    minus = minus.reshape(2 * FINE, seg_count, share, COARSE * chan)
    both = jnp.stack(
        [
            jnp.transpose(plus, (1, 0, 2, 3)).reshape(seg_count, -1, chan),
            jnp.transpose(minus, (1, 0, 2, 3)).reshape(seg_count, -1, chan),
        ],
        axis=1,
    )
    kept = lax.psum_scatter(both, "seg", scatter_dimension=0, tiled=True)[0]
    scaling = 1.0 / math.sqrt(frequencies * seg_all)
    own = kept[0].reshape(COARSE, share, 2 * FINE, chan)
    own = jnp.transpose(own, (1, 3, 0, 2)).reshape(share, chan, LH) * scaling
    other = kept[1].reshape(2 * FINE, share, COARSE, chan)[::-1]
    other = jnp.transpose(other, (1, 3, 2, 0)).reshape(share, chan, LH) * scaling
    others = lax.all_gather(other, "blk", axis=0)
    lead_here = lead[blk_index]
    came_from = take_small(owner, (lead_here ^ 1)[None])[0]
    got = lax.dynamic_index_in_dim(others, came_from, 0, keepdims=False)
    first = lead_here % 2 == 0
    return jnp.stack([jnp.where(first, own, got), jnp.where(first, got, own)])[None]


def solution(mesh):
    in_specs = (P(None, ("blk", "seg"), None, None), P(), P())
    out_specs = P(None, "blk", "seg", None, None)
    return jax.shard_map(local, mesh=mesh, in_specs=in_specs, out_specs=out_specs, check_vma=False)
```

time: 476 us -> 255 us (0.54)
  waiting for transfers between devices: 253 us -> 144 us
  other arithmetic: 85.7 us -> 11.2 us
  matrix products: 66.2 us -> 2.72 us
  Pallas kernels: 0 us -> 35.7 us
  local copies, waits for them, and re-layouts: 37.9 us -> 27.1 us
  between operations: 13.5 us -> 21 us
  loops' own time: 7.09 us -> 0 us
    psum x1 -> x0, waiting for transfers between devices: 95.9 us -> none  [local(): lax.psum(pair_terms(own_panels, others, lag_table, channels), 'seg')]
    dot_general x16 -> x1, matrix products: 66.2 us -> 2.72 us  [local(): jnp.dot(pack, column, preferred_element_type=jnp.float32)]
    another operation x3 -> x1, other arithmetic: 66.2 us -> 7.53 us  [local(): jnp.stack([jnp.transpose(plus, (1, 0, 2, 3)).reshape(seg_count, -1, chan)...]
    all_gather x1, waiting for transfers between devices: 77.6 us -> 22.7 us  [local(): others = lax.all_gather(other, 'blk', axis=0)]
    reduce_scatter x0 -> x1, waiting for transfers between devices: none -> 48.1 us  [local(): kept = lax.psum_scatter(both, 'seg', scatter_dimension=0, tiled=True)[0]]
    pallas_call x0 -> x1, Pallas kernels: none -> 35.7 us  [correlate(): pl.pallas_call(functools.partial(correlate_kernel, chan), grid=(frequenci...]
    gather x6 -> x0, local copies, waits for them, and re-layouts: 28.6 us -> none  [the longest x1 11 us: local(): jnp.take(column, outgoing.reshape(-1), axis=1, mode='fill', fill_value=0)]
    another operation x1 -> x3, local copies, waits for them, and re-layouts: 0.01 us -> 13.7 us  [local(): jnp.stack([jnp.transpose(plus, (1, 0, 2, 3)).reshape(seg_count, -1, chan)...]
  transfers between devices with their start and end apart: 4 -> 4, of which waited for: 4 -> 4; matrix products, arithmetic and copies ran while one was open for 3% -> 2% of each run, Pallas kernels for 0% -> 0%
where the time goes in v1:
time: 255 us; the launch traced here: 252 us
  waiting for transfers between devices  144 us (56%)
  Pallas kernels  35.7 us (14%)
  local copies, waits for them, and re-layouts  27.1 us (11%)
  between operations  21 us (8%)
  other arithmetic  11.2 us (4%)
  starting transfers between devices  10.4 us (4%)
  matrix products  2.72 us (1%)
    reduce_scatter x1, waiting for transfers between devices, local(): kept = lax.psum_scatter(both, 'seg', scatter_dimension=0, tiled=True)[0]  48.1 us
    all_to_all x1, waiting for transfers between devices, local(): lax.all_to_all(rows, 'seg', split_axis=0, concat_axis=0, tiled=True)  43.5 us
    pallas_call x1, Pallas kernels, correlate(): pl.pallas_call(functools.partial(correlate_kernel, chan), grid=(frequenci...  35.7 us
    all_to_all x1, waiting for transfers between devices, local(): lax.all_to_all(packed, 'blk', split_axis=0, concat_axis=0, tiled=True)  29.8 us
    all_gather x1, waiting for transfers between devices, local(): others = lax.all_gather(other, 'blk', axis=0)  22.7 us
    another operation x3, local copies, waits for them, and re-layouts, local(): jnp.stack([jnp.transpose(plus, (1, 0, 2, 3)).reshape(seg_count, -1, chan)...  13.7 us
    another operation x1, other arithmetic, local(): jnp.stack([jnp.transpose(plus, (1, 0, 2, 3)).reshape(seg_count, -1, chan)...  7.53 us
    all_to_all x1, starting transfers between devices, local(): lax.all_to_all(rows, 'seg', split_axis=0, concat_axis=0, tiled=True)  5.54 us
  transfers between devices with their start and end apart: 4, of which 4 were waited for; matrix products, arithmetic and copies ran while one was open for 2% of the time, Pallas kernels for 0%

profile of v1, /device:TPU:25, one launch (start us, length us, event | category | flops | bytes accessed | tf_op | source)
XLA Modules:
  0.0 252.4 jit_solution(13167824395276102325)
XLA Ops:
  6.5 4.2 %copy.25 = bf16[8,16,2,4096]{3,1,2,0:T(8,128)(2,1)} copy(bf16[8,16,2,4096]{3,2,1,0:T(2,128)(2,1)} %param.7) | data formatting | bytes 4194304 | tf_op args[0]
  10.8 5.5 %all-to-all-start = ((bf16[8,32,4096]{2,1,0:T(8,128)(2,1)}), bf16[8,32,4096]{2,1,0:T(8,128)(2,1)S(1)}, u32[]{:S(2)}, u32[]{:S(2)}) async-start(bf16[8,32,4096]{2,1,0:T(8,128)(2,1)} %bitcast.4), calls=%async_computation | async-start | bytes 4194304 | tf_op jit(solution)/shard_map/all_to_all | solution.py:165
  16.3 0.1 eq.216
  16.4 0.2 select_reduce_fusion.3
  16.6 0.2 select_reduce_fusion.2
  16.8 0.2 select_reduce_fusion.1
  17.0 0.1 broadcast_in_dim.111
  17.1 0.1 broadcast_in_dim.112
  17.1 0.2 select_reduce_fusion
  17.4 0.1 convert_reduce_fusion.1
  17.5 0.1 add.78
  17.6 0.2 broadcast_compare_fusion
  17.8 0.7 broadcast_and_fusion
  18.5 0.7 and.95
  19.3 43.5 %all-to-all-done = bf16[8,32,4096]{2,1,0:T(8,128)(2,1)S(1)} async-done(((bf16[8,32,4096]{2,1,0:T(8,128)(2,1)}), bf16[8,32,4096]{2,1,0:T(8,128)(2,1)S(1)}, u32[]{:S(2)}, u32[]{:S(2)}) %all-to-all-start) | async-done | bytes 2097184 | tf_op jit(solution)/shard_map/all_to_all | solution.py:165
  62.7 2.7 %convolution_convert_fusion = bf16[384,4096]{1,0:T(8,128)(2,1)} fusion(pred[384,256]{0,1:T(32,128)(4,1)S(1)} %and.95, bf16[256,4096]{1,0:T(8,128)(2,1)S(1)} %bitcast.73), kind=kOutput, calls=%fused_computation.1 | convolution fusion | flops 806879232 | bytes 5341184 | tf_op jit(solution)/shard_map/dot_general | solution.py:167
  65.5 4.8 %all-to-all-start.1 = ((bf16[4,96,4096]{2,1,0:T(8,128)(2,1)}), bf16[4,96,4096]{2,1,0:T(8,128)(2,1)}, u32[]{:S(2)}, u32[]{:S(2)}) async-start(bf16[4,96,4096]{2,1,0:T(8,128)(2,1)} %bitcast.70), calls=%async_computation.1 | async-start | bytes 6291456 | tf_op jit(solution)/shard_map/all_to_all | solution.py:169
  70.3 0.1 slice.11
  70.4 0.6 dynamic_slice.11
  72.1 0.2 select_reduce_fusion.5
  72.3 0.6 dynamic_slice.12
  75.4 0.1 and_select_fusion.1
  75.5 0.2 convert_reduce_fusion
  75.7 0.1 broadcast_compare_fusion.1
  75.8 0.3 and_convert_fusion
  76.1 0.2 copy.26.unpack
  76.3 29.8 %all-to-all-done.1 = bf16[4,96,4096]{2,1,0:T(8,128)(2,1)} async-done(((bf16[4,96,4096]{2,1,0:T(8,128)(2,1)}), bf16[4,96,4096]{2,1,0:T(8,128)(2,1)}, u32[]{:S(2)}, u32[]{:S(2)}) %all-to-all-start.1) | async-done | bytes 3145760 | tf_op jit(solution)/shard_map/all_to_all | solution.py:169
  106.1 35.7 %shard_map.55 = (f32[512,1024]{1,0:T(8,128)S(1)}, f32[1024,512]{1,0:T(8,128)S(1)}) custom-call(bf16[384,4096]{1,0:T(8,128)(2,1)} %bitcast.7.arrived, bf16[256,384]{1,0:T(8,128)(2,1)S(1)} %copy.26.unpack, f32[16,4096]{1,0:T(8,128)S(1)} %copy-done.1, f32[16,4096]{1,0:T(8,128)S(1)} %copy-done), custom_call_target="tpu_custom_call" | custom-call | flops 17179869184 | bytes 7340032 | tf_op jit(solution)/shard_map/pallas_call | solution.py:89
  141.8 0.1 copy.45
  142.0 1.6 copy.44
  143.6 4.4 %stack_reshape.7 = f32[8,1,1024,64]{3,2,0,1:T(8,128)} reshape(f32[8,16,8,512]{3,2,1,0:T(8,128)} %bitcast.72) | data formatting | bytes 4194304 | tf_op jit(solution)/shard_map/stack;reshape | solution.py:175
  147.9 2.5 stack_reshape.6
  150.5 7.5 %pad_maximum_fusion = f32[8,2,1024,64]{3,2,0,1:T(8,128)} fusion(f32[8,1,1024,64]{3,2,0,1:T(8,128)} %stack_reshape.7, f32[8,1,1024,64]{3,2,0,1:T(8,128)} %stack_reshape.6), kind=kLoop, calls=%fused_computation | loop fusion | flops 1048576 | bytes 8388608 | tf_op jit(solution)/shard_map/stack | solution.py:175
  158.0 6.8 %copy.29 = f32[8,2,1024,64]{2,3,1,0:T(8,128)} copy(f32[8,2,1024,64]{3,2,0,1:T(8,128)} %pad_maximum_fusion) | data formatting | bytes 8388608 | tf_op jit(solution)/shard_map/stack | solution.py:175
  164.9 48.1 %reduce-scatter.2.cloned.1.call-done = f32[1,2,1024,64]{2,3,1,0:T(8,128)} async-done(((f32[8,2,1024,64]{2,3,1,0:T(8,128)}), f32[1,2,1024,64]{2,3,1,0:T(8,128)}) %reduce-scatter.2.cloned.1.call-update) | async-done | bytes 524304 | tf_op jit(solution)/shard_map/reduce_scatter | solution.py:182
  213.0 1.1 fusion.6
  214.1 0.2 copy.38
  214.3 0.1 multiply_bitcast_fusion
  214.3 0.3 copy.33
  214.7 0.9 copy.34
  216.1 0.7 fusion.4
  220.1 0.2 copy.37
  220.4 22.7 %all-gather.2.cloned.1.call-done = f32[4,8,64,128]{3,2,1,0:T(8,128)} async-done(((f32[1,8,64,128]{3,2,1,0:T(8,128)}), f32[4,8,64,128]{3,2,1,0:T(8,128)}) %all-gather.2.cloned.1.call-update) | async-done | bytes 1048592 | tf_op jit(solution)/shard_map/all_gather | solution.py:188
  243.1 1.0 constant_dynamic-slice_fusion.2
  244.1 0.2 copy.39
  244.3 0.1 bitcast_select_fusion.1
  244.4 0.1 maximum_bitcast_fusion
  244.5 1.1 copy.36
  (27 shorter events, 0.3 us)
Async XLA Ops:
  10.8 5.6 %copy-start.2 = (s32[8,64]{1,0:T(8,128)S(1)}, s32[8,64]{1,0:T(8,128)}, u32[]{:S(2)}) copy-start(s32[8,64]{1,0:T(8,128)} %param.8) | copy-start | bytes 6148
  10.8 5.6 %copy-start.3 = (s32[1,8]{1,0:T(1,128)S(1)}, s32[1,8]{1,0:T(1,128)}, u32[]{:S(2)}) copy-start(s32[1,8]{1,0:T(1,128)} %param.9) | copy-start | bytes 100
  10.8 52.0 %all-to-all-start = ((bf16[8,32,4096]{2,1,0:T(8,128)(2,1)}), bf16[8,32,4096]{2,1,0:T(8,128)(2,1)S(1)}, u32[]{:S(2)}, u32[]{:S(2)}) async-start(bf16[8,32,4096]{2,1,0:T(8,128)(2,1)} %bitcast.4), calls=%async_computation | async-start | bytes 4194304 | tf_op jit(solution)/shard_map/all_to_all | solution.py:165
  65.5 40.6 %copy-start = (f32[16,4096]{1,0:T(8,128)S(1)}, f32[16,4096]{1,0:T(8,128)}, u32[]{:S(2)}) copy-start(f32[16,4096]{1,0:T(8,128)} %constant.79.clone.sin_ref) | copy-start | bytes 786436
  65.5 40.6 %copy-start.1 = (f32[16,4096]{1,0:T(8,128)S(1)}, f32[16,4096]{1,0:T(8,128)}, u32[]{:S(2)}) copy-start(f32[16,4096]{1,0:T(8,128)} %constant.78.clone.cos_ref) | copy-start | bytes 786436
  65.5 40.6 %all-to-all-start.1 = ((bf16[4,96,4096]{2,1,0:T(8,128)(2,1)}), bf16[4,96,4096]{2,1,0:T(8,128)(2,1)}, u32[]{:S(2)}, u32[]{:S(2)}) async-start(bf16[4,96,4096]{2,1,0:T(8,128)(2,1)} %bitcast.70), calls=%async_computation.1 | async-start | bytes 6291456 | tf_op jit(solution)/shard_map/all_to_all | solution.py:169
  70.2 142.8 %reduce-scatter.2.cloned.1.call-start = ((), (), s32[]{:S(2)}) async-start(), calls=%async_computation.3 | async-start | bytes 4718592 | tf_op jit(solution)/shard_map/reduce_scatter | solution.py:182
  164.8 78.3 %all-gather.2.cloned.1.call-start = ((), (), s32[]{:S(2)}) async-start(), calls=%async_computation.4 | async-start | bytes 1310720 | tf_op jit(solution)/shard_map/all_gather | solution.py:188
Sparse Core Ops, SparseCore 0:
  164.9 48.0 reduce-scatter.1
  215.7 27.3 all-gather.1

commit v2 on v1

v2 whole, which is shorter than its diff:
```python
import functools
import math

import numpy as np
import jax
import jax.numpy as jnp
from jax import lax
from jax.experimental import pallas as pl
from jax.experimental.pallas import tpu as pltpu
from jax.sharding import PartitionSpec as P

LH = 128
STEP = 16
COARSE = LH // STEP
FINE = STEP // 2
CHUNK = 512
NT = (((1,), (1,)), ((), ()))


def phase_tables(frequencies):
    freq = np.arange(frequencies, dtype=np.float64)[None, :]
    coarse = (STEP * np.arange(COARSE, dtype=np.float64) + (STEP - 1) / 2)[:, None]
    fine = (np.arange(FINE, dtype=np.float64) + 0.5)[:, None]
    angles = np.concatenate([coarse, fine], 0) * freq * (math.pi / frequencies)
    return np.cos(angles).astype(np.float32), np.sin(angles).astype(np.float32)


def take_small(table, index):
    hit = index[:, None] == jnp.arange(table.shape[0], dtype=jnp.int32)[None, :]
    return jnp.sum(jnp.where(hit, table[None, :], 0), axis=1)


def assign(partner):
    count = partner.shape[0]
    blocks = jnp.arange(count, dtype=jnp.int32)
    hop = partner ^ 1
    lowest = blocks
    for _ in range(max(1, (count // 2 - 1).bit_length())):
        lowest = jnp.minimum(lowest, take_small(lowest, hop))
        hop = take_small(hop, hop)
    return lowest < take_small(lowest, blocks ^ 1)


def fused_kernel(
    chan, bound, tail, rows_ref, pack, unpack, cos_ref, sin_ref, *rest
):
    if tail:
        own_ref, others_ref, *rest = rest
    else:
        plus_out, minus_out, *rest = rest
    col, packed, arr, xp, xm, yp, plus, minus, a_send, a_recv, b_send, b_recv, local_sem, *rest = rest
    blk_count, seg_count = lax.axis_size("blk"), lax.axis_size("seg")
    blk, seg = lax.axis_index("blk"), lax.axis_index("seg")
    chunks = col.shape[0]
    held = rows_ref.shape[1]
    width = col.shape[2]
    bf = jnp.bfloat16
    mesh_ids = pl.DeviceIdType.MESH

    def seg_peer(step):
        return lax.rem(seg + step, seg_count)

    def blk_peer(step):
        return lax.rem(blk + step, blk_count)

    barrier = pltpu.get_barrier_semaphore()
    for step in range(1, seg_count):
        pl.semaphore_signal(barrier, inc=1, device_id=(blk, seg_peer(step)), device_id_type=mesh_ids)
    for step in range(1, blk_count):
        pl.semaphore_signal(barrier, inc=1, device_id=(blk_peer(step), seg), device_id_type=mesh_ids)
    pl.semaphore_wait(barrier, seg_count + blk_count - 2)

    def a_copy(k, step):
        to = seg_peer(step)
        return pltpu.make_async_remote_copy(
            src_ref=rows_ref.at[to, :, pl.ds(pl.multiple_of(k * width, width), width)],
            dst_ref=col.at[k, pl.ds(pl.multiple_of(seg * held, held), held), :],
            send_sem=a_send.at[k, step],
            recv_sem=a_recv.at[k, step],
            device_id=(blk, to),
            device_id_type=mesh_ids,
        )

    def a_own(k):
        return pltpu.make_async_copy(
            rows_ref.at[seg, :, pl.ds(pl.multiple_of(k * width, width), width)],
            col.at[k, pl.ds(pl.multiple_of(seg * held, held), held), :],
            local_sem.at[k],
        )

    def b_copy(k, step):
        to = blk_peer(step)
        return pltpu.make_async_remote_copy(
            src_ref=packed.at[k, to],
            dst_ref=arr.at[k, blk],
            send_sem=b_send.at[k, step],
            recv_sem=b_recv.at[k, step],
            device_id=(to, seg),
            device_id_type=mesh_ids,
        )

    def b_own(k):
        return pltpu.make_async_copy(packed.at[k, blk], arr.at[k, blk], b_send.at[k, 0])

    @pl.loop(0, chunks)
    def _(k):
        for step in range(1, seg_count):
            a_copy(k, step).start()
        a_own(k).start()

    plus[...] = jnp.zeros_like(plus)
    minus[...] = jnp.zeros_like(minus)

    def route(k):
        for step in range(1, seg_count):
            a_copy(k, step).wait_recv()
        a_own(k).wait()
        mixed = jnp.dot(pack[...], col[k], preferred_element_type=jnp.float32).astype(bf)
        packed[k] = mixed.reshape(blk_count, 2 * bound, width)
        for step in range(1, blk_count):
            b_copy(k, step).start()
        b_own(k).start()

    def work(k):
        for step in range(1, blk_count):
            b_copy(k, step).wait_recv()
        b_own(k).wait()
        block = arr[k].reshape(blk_count * 2 * bound, width)
        rows = jnp.dot(unpack[...], block, preferred_element_type=jnp.float32)
        xr, yr = rows[0:chan], rows[chan : 2 * chan]
        xi, yi = rows[2 * chan : 3 * chan], rows[3 * chan : 4 * chan]
        re, im = pl.ds(0, width), pl.ds(width, width)
        for a in range(COARSE):
            c, s = cos_ref[k, a : a + 1, :], sin_ref[k, a : a + 1, :]
            rc, rs, ic, i_s = xr * c, xr * s, xi * c, xi * s
            at = pl.ds(a * chan, chan)
            xp[at, re] = (rc - i_s).astype(bf)
            xp[at, im] = (ic + rs).astype(bf)
            xm[at, re] = (rc + i_s).astype(bf)
            xm[at, im] = (ic - rs).astype(bf)
        for m in range(COARSE, COARSE + FINE):
            c, s = cos_ref[k, m : m + 1, :], sin_ref[k, m : m + 1, :]
            rc, rs, ic, i_s = yr * c, yr * s, yi * c, yi * s
            at, back = pl.ds((FINE + m - COARSE) * chan, chan), pl.ds((FINE - 1 - m + COARSE) * chan, chan)
            yp[at, re] = (rc + i_s).astype(bf)
            yp[at, im] = (ic - rs).astype(bf)
            yp[back, re] = (rc - i_s).astype(bf)
            yp[back, im] = (ic + rs).astype(bf)
        tile = 4 * chan

        @pl.loop(0, yp.shape[0] // tile)
        def _(t):
            at = pl.ds(pl.multiple_of(t * tile, tile), tile)
            y = yp[at, :]
            first = lax.dot_general(xp[...], y, NT, preferred_element_type=jnp.float32)
            plus[:, :, at] += first.reshape(COARSE, chan, tile)
            second = lax.dot_general(y, xm[...], NT, preferred_element_type=jnp.float32)
            minus[pl.ds(t * 4, 4)] += second.reshape(4, chan, COARSE * chan)

    route(0)

    @pl.loop(1, chunks)
    def _(k):
        route(k)
        work(k - 1)

    work(chunks - 1)

    if tail:
        from_core_m, from_core_p, stage_m, stage_p, from_z_m, from_z_p, done, c_send, c_recv, z_send, z_recv, o_send, o_recv, own_sem = rest
        share = chan // seg_count
        z_count = seg_count // 2
        core, z = lax.rem(seg, 2), lax.div(seg, 2)
        sides = ((minus, from_core_m, stage_m, from_z_m), (plus, from_core_p, stage_p, from_z_p))

        def z_peer(step):
            return lax.rem(z + step, z_count)

        def rows_of(target):
            return pl.ds(pl.multiple_of(target * share, share), share)

        def c_copy(side, step):
            acc, landing, _, _ = sides[side]
            to_z = z_peer(step)
            return pltpu.make_async_remote_copy(
                src_ref=acc.at[:, rows_of(2 * to_z + 1 - core), :],
                dst_ref=landing.at[step],
                send_sem=c_send.at[side, step],
                recv_sem=c_recv.at[side, step],
                device_id=(blk, 2 * z + 1 - core),
                device_id_type=mesh_ids,
            )

        def z_copy(side, step):
            _, _, stage, landing = sides[side]
            return pltpu.make_async_remote_copy(
                src_ref=stage.at[step],
                dst_ref=landing.at[step],
                send_sem=z_send.at[side, step],
                recv_sem=z_recv.at[side, step],
                device_id=(blk, 2 * z_peer(step) + core),
                device_id_type=mesh_ids,
            )

        order = list(range(1, z_count)) + [0]
        for side in range(2):
            for step in order:
                c_copy(side, step).start()
        for side in range(2):
            acc, landing, stage, _ = sides[side]
            for step in order[:-1]:
                c_copy(side, step).wait_recv()
                both = acc[:, rows_of(2 * z_peer(step) + core), :] + landing[step]
                stage[step] = both.reshape(-1, both.shape[-1]).astype(bf)
                z_copy(side, step).start()

        def finish(side):
            acc, landing, _, terms = sides[side]
            c_copy(side, 0).wait_recv()
            total = acc[:, rows_of(seg), :] + landing[0]
            for step in range(1, z_count):
                z_copy(side, step).wait_recv()
                total = total + terms[step].astype(jnp.float32).reshape(total.shape)
            return total

        def o_copy(step):
            return pltpu.make_async_remote_copy(
                src_ref=done,
                dst_ref=others_ref.at[blk],
                send_sem=o_send.at[step],
                recv_sem=o_recv.at[step],
                device_id=(blk_peer(step), seg),
                device_id_type=mesh_ids,
            )

        keep = pltpu.make_async_copy(done, others_ref.at[blk], own_sem)
        done[...] = finish(0)
        for step in range(1, blk_count):
            o_copy(step).start()
        keep.start()
        own_ref[...] = finish(1)
        keep.wait()
        for step in range(1, blk_count):
            o_copy(step).wait()
        for side in range(2):
            for step in order:
                c_copy(side, step).wait_send()
            for step in order[:-1]:
                z_copy(side, step).wait_send()
    else:
        plus_out[...] = plus[...]
        minus_out[...] = minus[...]

    @pl.loop(0, chunks)
    def _(k):
        for step in range(1, seg_count):
            a_copy(k, step).wait_send()
        for step in range(1, blk_count):
            b_copy(k, step).wait_send()


def correlate(rows, pack, unpack, chan, bound, tail):
    _, held, frequencies = rows.shape
    blk_count, seg_count = lax.axis_size("blk"), lax.axis_size("seg")
    chunks = frequencies // CHUNK
    cos, sin = phase_tables(frequencies)

    def by_chunk(table):
        return np.ascontiguousarray(table.reshape(-1, chunks, CHUNK).transpose(1, 0, 2))

    wide = COARSE * chan
    f32, bf = jnp.float32, jnp.bfloat16
    share = chan // seg_count
    z_count = seg_count // 2
    plus_shape, minus_shape = (COARSE, chan, 2 * wide), (2 * FINE, chan, wide)
    p_shape, m_shape = (COARSE, share, 2 * wide), (2 * FINE, share, wide)
    dma = pltpu.SemaphoreType.DMA
    in_vmem, anywhere = pl.BlockSpec(memory_space=pltpu.VMEM), pl.BlockSpec(memory_space=pl.ANY)
    scratch = [
        pltpu.VMEM((chunks, seg_count * held, CHUNK), bf),
        pltpu.VMEM((chunks, blk_count, 2 * bound, CHUNK), bf),
        pltpu.VMEM((chunks, blk_count, 2 * bound, CHUNK), bf),
        pltpu.VMEM((wide, 2 * CHUNK), bf),
        pltpu.VMEM((wide, 2 * CHUNK), bf),
        pltpu.VMEM((2 * wide, 2 * CHUNK), bf),
        pltpu.VMEM(plus_shape, f32),
        pltpu.VMEM(minus_shape, f32),
        dma((chunks, seg_count)),
        dma((chunks, seg_count)),
        dma((chunks, blk_count)),
        dma((chunks, blk_count)),
        dma((chunks,)),
    ]
    if tail:
        out_shape = [jax.ShapeDtypeStruct(p_shape, f32), jax.ShapeDtypeStruct((blk_count,) + m_shape, f32)]
        out_specs = [in_vmem, anywhere]
        flat_p, flat_m = (COARSE * share, 2 * wide), (2 * FINE * share, wide)
        scratch += [
            pltpu.VMEM((z_count,) + m_shape, f32),
            pltpu.VMEM((z_count,) + p_shape, f32),
            pltpu.VMEM((z_count,) + flat_m, bf),
            pltpu.VMEM((z_count,) + flat_p, bf),
            pltpu.VMEM((z_count,) + flat_m, bf),
            pltpu.VMEM((z_count,) + flat_p, bf),
            pltpu.VMEM(m_shape, f32),
            dma((2, z_count)),
            dma((2, z_count)),
            dma((2, z_count)),
            dma((2, z_count)),
            dma((blk_count,)),
            dma((blk_count,)),
            dma(()),
        ]
    else:
        out_shape = [jax.ShapeDtypeStruct(plus_shape, f32), jax.ShapeDtypeStruct(minus_shape, f32)]
        out_specs = [in_vmem, in_vmem]
    return pl.pallas_call(
        functools.partial(fused_kernel, chan, bound, tail),
        in_specs=[anywhere] + [in_vmem] * 4,
        out_specs=out_specs,
        out_shape=out_shape,
        scratch_shapes=scratch,
        compiler_params=pltpu.CompilerParams(
            collective_id=0, has_side_effects=True, vmem_limit_bytes=56 * 1024 * 1024
        ),
        cost_estimate=pl.CostEstimate(
            flops=8 * wide * wide * frequencies * 2, bytes_accessed=16 * wide * wide, transcendentals=0
        ),
    )(rows, pack, unpack, by_chunk(cos), by_chunk(sin))


def local(spectra, fibre_lists, pairing):
    seg_all, held, _, frequencies = spectra.shape
    blk_count = lax.axis_size("blk")
    seg_count = lax.axis_size("seg")
    blk_index = lax.axis_index("blk")
    block_count, chan = fibre_lists.shape
    width = held * seg_count
    bound = 2 * (3 * chan // (2 * blk_count))
    partner = pairing[0]

    blocks = jnp.arange(block_count, dtype=jnp.int32)
    leads = assign(partner)
    owner = jnp.where(leads, blocks, partner) // 2
    lead_parity = (~leads[0::2]).astype(jnp.int32)
    lead = 2 * jnp.arange(blk_count, dtype=jnp.int32) + lead_parity
    follow = take_small(partner, lead)
    i32 = jnp.int32

    mine = blk_index * width + jnp.arange(width, dtype=i32)
    flat = fibre_lists.reshape(-1)
    flat_owner = jnp.repeat(owner, chan)
    pair_of = jnp.sum(jnp.where(flat[:, None] == mine[None, :], flat_owner[:, None], 0), axis=0)
    order = jnp.arange(width, dtype=i32)
    rank = jnp.sum((pair_of[:, None] == pair_of[None, :]) & (order[:, None] < order[None, :]), axis=0).astype(i32)
    spot = pair_of * bound + rank
    hit = jnp.arange(blk_count * bound, dtype=i32)[:, None] == spot[None, :]
    hit = hit.reshape(blk_count, 1, bound, seg_count, 1, held)
    part = jnp.arange(2, dtype=i32)
    same = (part[:, None] == part[None, :]).reshape(1, 2, 1, 1, 2, 1)
    pack = (hit & same).astype(jnp.bfloat16).reshape(blk_count * 2 * bound, 2 * width)

    pair = jnp.concatenate(
        [jnp.take(fibre_lists, lead[blk_index], axis=0), jnp.take(fibre_lists, follow[blk_index], axis=0)]
    )
    source = pair // width
    rank = jnp.sum((source[:, None] == source[None, :]) & (pair[None, :] < pair[:, None]), axis=1).astype(i32)
    spot = source * bound + rank
    hit = spot[:, None] == jnp.arange(blk_count * bound, dtype=i32)[None, :]
    hit = hit.reshape(1, 2 * chan, blk_count, 1, bound)
    same = (part[:, None] == part[None, :]).reshape(2, 1, 1, 2, 1)
    unpack = (hit & same).astype(jnp.bfloat16).reshape(4 * chan, blk_count * 2 * bound)

    rows = jnp.transpose(spectra, (0, 2, 1, 3)).reshape(seg_all, 2 * held, frequencies)
    share = chan // seg_count
    tail = share % 8 == 0
    plus, minus = correlate(rows, pack, unpack, chan, bound, tail)
    lead_here = lead[blk_index]
    came_from = take_small(owner, (lead_here ^ 1)[None])[0]
    scaling = 1.0 / math.sqrt(frequencies * seg_all)
    if tail:
        other = lax.dynamic_index_in_dim(minus, came_from, 0, keepdims=False)
    else:
        plus = lax.psum_scatter(plus, "seg", scatter_dimension=1, tiled=True)
        other = lax.psum_scatter(minus, "seg", scatter_dimension=1, tiled=True)
        others = lax.all_gather(other, "blk", axis=0)
        other = lax.dynamic_index_in_dim(others, came_from, 0, keepdims=False)
    own = plus.reshape(COARSE, share, 2 * FINE, chan)
    own = jnp.transpose(own, (1, 3, 0, 2)).reshape(share, chan, LH) * scaling
    got = other.reshape(2 * FINE, share, COARSE, chan)[::-1]
    got = jnp.transpose(got, (1, 3, 2, 0)).reshape(share, chan, LH) * scaling
    first = lead_here % 2 == 0
    return jnp.stack([jnp.where(first, own, got), jnp.where(first, got, own)])[None]


def solution(mesh):
    in_specs = (P(None, ("blk", "seg"), None, None), P(), P())
    out_specs = P(None, "blk", "seg", None, None)
    return jax.shard_map(local, mesh=mesh, in_specs=in_specs, out_specs=out_specs, check_vma=False)
```

time: 255 us -> 136 us (0.53)
  waiting for transfers between devices: 144 us -> 0 us
  Pallas kernels: 35.7 us -> 108 us
  local copies, waits for them, and re-layouts: 27.1 us -> 9.96 us
  between operations: 21 us -> 8.04 us
  starting transfers between devices: 10.4 us -> 0 us
  matrix products: 2.72 us -> 0 us
    all_to_all x2 -> x0, waiting for transfers between devices: 73.3 us -> none  [the longest x1 43.5 us: local(): lax.all_to_all(rows, 'seg', split_axis=0, concat_axis=0, tiled=True)]
    pallas_call x1, Pallas kernels: 35.7 us -> 108 us  [correlate(): pl.pallas_call(functools.partial(fused_kernel, chan, bound, tail), in_spe...]
    reduce_scatter x1 -> x0, waiting for transfers between devices: 48.1 us -> none  [local(): kept = lax.psum_scatter(both, 'seg', scatter_dimension=0, tiled=True)[0]]
    all_gather x1 -> x0, waiting for transfers between devices: 22.7 us -> none  [local(): others = lax.all_gather(other, 'blk', axis=0)]
    another operation x3 -> x0, local copies, waits for them, and re-layouts: 13.7 us -> none  [local(): jnp.stack([jnp.transpose(plus, (1, 0, 2, 3)).reshape(seg_count, -1, chan)...]
    all_to_all x2 -> x0, starting transfers between devices: 10.3 us -> none  [the longest x1 5.54 us: local(): lax.all_to_all(rows, 'seg', split_axis=0, concat_axis=0, tiled=True)]
    another operation x1 -> x0, other arithmetic: 7.53 us -> none  [local(): jnp.stack([jnp.transpose(plus, (1, 0, 2, 3)).reshape(seg_count, -1, chan)...]
    unnamed x13 -> x3, local copies, waits for them, and re-layouts: 4.87 us -> 0.03 us
  transfers between devices with their start and end apart: 4 -> 0, of which waited for: 4 -> 0; matrix products, arithmetic and copies ran while one was open for 2% -> 0% of each run, Pallas kernels for 0% -> 0%
where the time goes in v2:
time: 136 us; the launch traced here: 135 us
  Pallas kernels  108 us (79%)
  local copies, waits for them, and re-layouts  9.96 us (7%)
  other arithmetic  9 us (7%)
  between operations  8.04 us (6%)
    pallas_call x1, Pallas kernels, correlate(): pl.pallas_call(functools.partial(fused_kernel, chan, bound, tail), in_spe...  108 us
    reduce_sum x5, other arithmetic, take_small(): return jnp.sum(jnp.where(hit, table[None, :], 0), axis=1)  2.78 us

profile of v2, /device:TPU:25, one launch (start us, length us, event | category | flops | bytes accessed | tf_op | source)
XLA Modules:
  0.0 135.4 jit_solution(11662740816646950713)
XLA Ops:
  0.0 0.0 copy-start
  0.0 0.8 broadcast_xor_fusion
  0.8 0.7 xor_bitcast_fusion
  1.5 0.2 select_reduce_fusion.3
  1.7 0.2 select_reduce_fusion.2
  1.9 0.2 select_reduce_fusion.1
  2.0 0.7 and_select_fusion.2
  2.7 0.1 slice.3
  2.8 0.6 dynamic_slice.11
  4.7 1.4 %fusion.4 = s32[]{:T(128)} fusion(s32[1,8]{1,0:T(1,128)} %param.9, s32[8]{0:T(128)S(1)} %select_reduce_fusion.1, s32[8]{0:T(128)S(1)} %select_reduce_fusion.2, s32[8]{0:T(128)S(1)} %get-tuple-element.22, s32[]{:T(128)S(6)} %xor.23), kind=kLoop, calls=%fused_computation.49 | loop fusion | flops 175 | bytes 136 | tf_op jit(solution)/shard_map/reduce_sum | solution.py:30
  10.8 0.8 select_reduce_fusion.5
  11.6 0.6 dynamic_slice.12
  14.1 0.8 fusion.1
  14.9 0.1 and_select_fusion.1
  15.0 0.2 convert_reduce_fusion
  15.2 0.8 eq.216
  16.0 0.1 broadcast_in_dim.111
  16.0 0.1 broadcast_in_dim.112
  16.1 0.2 select_reduce_fusion
  16.3 0.1 convert_reduce_fusion.1
  16.5 0.1 add.76
  16.5 0.1 broadcast_compare_fusion.1
  16.6 0.2 broadcast_compare_fusion
  16.9 0.3 and_convert_fusion.1
  17.1 0.8 copy.18.unpack
  18.0 0.7 and_convert_fusion
  18.7 0.4 reshape.420
  19.1 0.8 copy.17.pack
  19.9 0.0 copy-done
  19.9 2.7 %copy.16 = bf16[8,2,16,4096]{3,2,1,0:T(8,128)(2,1)} copy(bf16[8,2,16,4096]{3,1,2,0:T(2,128)(2,1)S(1)} %bitcast.50) | data formatting | bytes 4194304 | tf_op jit(solution)/shard_map/transpose | solution.py:374
  22.6 108.4 %shard_map.55 = (f32[8,8,1024]{2,1,0:T(8,128)}, f32[4,16,8,512]{3,2,1,0:T(8,128)}) custom-call(bf16[8,32,4096]{2,1,0:T(8,128)(2,1)} %bitcast.51, bf16[384,256]{1,0:T(8,128)(2,1)} %copy.17.pack, bf16[256,384]{1,0:T(8,128)(2,1)} %copy.18.unpack, f32[8,16,512]{2,1,0:T(8,128)} %constant.78.clone.cos_ref, f32[8,16,512]{2,1,0:T(8,128)} %constant.79.clone.sin_ref), custom_call_target="tpu_custom_call" | custom-call | flops 17179869184 | bytes 4194304 | tf_op jit(solution)/shard_map/pallas_call | solution.py:317
  131.0 1.0 broadcast_multiply_fusion
  132.0 1.0 constant_dynamic-slice_fusion.2
  133.0 0.1 reshape.382
  133.1 0.1 mul.65
  133.2 0.4 bitcast_select_fusion.1
  133.6 0.3 copy.20
  133.9 0.3 copy.21
  134.2 0.1 maximum_bitcast_fusion
  134.3 1.1 copy.22
  (9 shorter events, 0.1 us)
Async XLA Ops:
  0.0 19.9 %copy-start = (bf16[8,16,2,4096]{3,2,1,0:T(2,128)(2,1)S(1)}, bf16[8,16,2,4096]{3,2,1,0:T(2,128)(2,1)}, u32[]{:S(2)}) copy-start(bf16[8,16,2,4096]{3,2,1,0:T(2,128)(2,1)} %param.7) | copy-start | bytes 6291460

commit v3 on v2

--- a/solution.py
+++ b/solution.py
@@ -25,30 +25,76 @@
     return np.cos(angles).astype(np.float32), np.sin(angles).astype(np.float32)
 
 
-def take_small(table, index):
-    hit = index[:, None] == jnp.arange(table.shape[0], dtype=jnp.int32)[None, :]
-    return jnp.sum(jnp.where(hit, table[None, :], 0), axis=1)
-
-
-def assign(partner):
-    count = partner.shape[0]
-    blocks = jnp.arange(count, dtype=jnp.int32)
-    hop = partner ^ 1
-    lowest = blocks
-    for _ in range(max(1, (count // 2 - 1).bit_length())):
-        lowest = jnp.minimum(lowest, take_small(lowest, hop))
-        hop = take_small(hop, hop)
-    return lowest < take_small(lowest, blocks ^ 1)
+def plan(chan, bound, width, blk, blk_count, pairing, lists, lists_t, places, pack, unpack, chosen):
+    count = lists.shape[0]
+    i32, f32, bf = jnp.int32, jnp.float32, jnp.bfloat16
+
+    def lowest(block):
+        least = block
+        at = block
+        for _ in range(count // 2 - 1):
+            at = pairing[0, at] ^ 1
+            least = jnp.minimum(least, at)
+        return least
+
+    least = [lowest(jnp.int32(b)) for b in range(count)]
+    owner = [
+        jnp.where(least[b] < least[b ^ 1], jnp.int32(b), pairing[0, b]) // 2 for b in range(count)
+    ]
+    lead = jnp.int32(0)
+    came_from = jnp.int32(0)
+    for k in range(blk_count):
+        first = least[2 * k] < least[2 * k + 1]
+        lead = jnp.where(blk == k, jnp.where(first, 2 * k, 2 * k + 1), lead)
+        came_from = jnp.where(blk == k, jnp.where(first, owner[2 * k + 1], owner[2 * k]), came_from)
+    follow = pairing[0, lead]
+    chosen[0] = came_from
+    chosen[1] = lead % 2
+
+    columns = places.shape[1]
+    number = places[0:1, :]
+    pair_of = jnp.zeros((1, columns), i32)
+    for b in range(count):
+        hit = lists_t[:, b : b + 1] == number + blk * width
+        pair_of = pair_of + jnp.sum(jnp.where(hit, owner[b], 0), axis=0, keepdims=True)
+    kinds = max(8, blk_count)
+    real = (lax.broadcasted_iota(i32, (kinds, columns), 0) == pair_of) & (places[1:2, :] == 0)
+    before = places[2 : 2 + columns, :] < number
+    ranks = jnp.dot(
+        jnp.where(real, 1.0, 0.0).astype(bf),
+        jnp.where(before, 1.0, 0.0).astype(bf),
+        preferred_element_type=f32,
+    )
+    mine = lax.broadcasted_iota(i32, (kinds, columns), 0) == pair_of
+    rank = jnp.sum(jnp.where(mine, ranks, 0.0), axis=0, keepdims=True).astype(i32)
+    target = pair_of * (2 * bound) + places[1:2, :] * bound + rank
+    pack[...] = jnp.where(lax.broadcasted_iota(i32, pack.shape, 0) == target, 1.0, 0.0).astype(bf)
+
+    roles = (lead, follow)
+    zero_col, zero_row = jnp.zeros((chan, 1), i32), jnp.zeros((1, chan), i32)
+    tall = [sum((jnp.where(role == b, lists_t[:, b : b + 1], 0) for b in range(count)), zero_col) for role in roles]
+    flat = [sum((jnp.where(role == b, lists[b : b + 1, :], 0) for b in range(count)), zero_row) for role in roles]
+    shift = width.bit_length() - 1
+    lane = lax.broadcasted_iota(i32, (chan, unpack.shape[1]), 1)
+    for r in range(2):
+        rank = zero_col
+        for other in flat:
+            ahead = ((tall[r] >> shift) == (other >> shift)) & (other < tall[r])
+            rank = rank + jnp.sum(jnp.where(ahead, 1, 0), axis=1, keepdims=True)
+        spot = (tall[r] >> shift) * (2 * bound) + rank
+        for part in range(2):
+            hit = lane == spot + part * bound
+            unpack[(2 * part + r) * chan : (2 * part + r + 1) * chan, :] = jnp.where(hit, 1.0, 0.0).astype(bf)
 
 
 def fused_kernel(
-    chan, bound, tail, rows_ref, pack, unpack, cos_ref, sin_ref, *rest
+    chan, bound, tail, rows_ref, pairing, lists, lists_t, places, cos_ref, sin_ref, *rest
 ):
     if tail:
-        own_ref, others_ref, *rest = rest
+        own_ref, others_ref, chosen, *rest = rest
     else:
-        plus_out, minus_out, *rest = rest
-    col, packed, arr, xp, xm, yp, plus, minus, a_send, a_recv, b_send, b_recv, local_sem, *rest = rest
+        plus_out, minus_out, chosen, *rest = rest
+    pack, unpack, col, packed, arr, xp, xm, yp, plus, minus, a_send, a_recv, b_send, b_recv, local_sem, *rest = rest
     blk_count, seg_count = lax.axis_size("blk"), lax.axis_size("seg")
     blk, seg = lax.axis_index("blk"), lax.axis_index("seg")
     chunks = col.shape[0]
@@ -110,6 +156,7 @@
 
     plus[...] = jnp.zeros_like(plus)
     minus[...] = jnp.zeros_like(minus)
+    plan(chan, bound, seg_count * held // 2, blk, blk_count, pairing, lists, lists_t, places, pack, unpack, chosen)
 
     def route(k):
         for step in range(1, seg_count):
@@ -259,14 +306,21 @@
             b_copy(k, step).wait_send()
 
 
-def correlate(rows, pack, unpack, chan, bound, tail):
-    _, held, frequencies = rows.shape
+def correlate(rows, pairing, fibre_lists, bound, tail):
+    held, frequencies = rows.shape[1], rows.shape[2]
+    chan = fibre_lists.shape[1]
     blk_count, seg_count = lax.axis_size("blk"), lax.axis_size("seg")
     chunks = frequencies // CHUNK
     cos, sin = phase_tables(frequencies)
 
     def by_chunk(table):
         return np.ascontiguousarray(table.reshape(-1, chunks, CHUNK).transpose(1, 0, 2))
+
+    slots = np.arange(seg_count * held)
+    number = slots // held * (held // 2) + slots % (held // 2)
+    part = slots // (held // 2) % 2
+    across = np.broadcast_to(number[:, None], (slots.size, slots.size))
+    places = np.concatenate([number[None], part[None], across]).astype(np.int32)
 
     wide = COARSE * chan
     f32, bf = jnp.float32, jnp.bfloat16
@@ -276,7 +330,10 @@
     p_shape, m_shape = (COARSE, share, 2 * wide), (2 * FINE, share, wide)
     dma = pltpu.SemaphoreType.DMA
     in_vmem, anywhere = pl.BlockSpec(memory_space=pltpu.VMEM), pl.BlockSpec(memory_space=pl.ANY)
+    in_smem, picked = pl.BlockSpec(memory_space=pltpu.SMEM), jax.ShapeDtypeStruct((2,), jnp.int32)
     scratch = [
+        pltpu.VMEM((blk_count * 2 * bound, seg_count * held), bf),
+        pltpu.VMEM((4 * chan, blk_count * 2 * bound), bf),
         pltpu.VMEM((chunks, seg_count * held, CHUNK), bf),
         pltpu.VMEM((chunks, blk_count, 2 * bound, CHUNK), bf),
         pltpu.VMEM((chunks, blk_count, 2 * bound, CHUNK), bf),
@@ -292,8 +349,8 @@
         dma((chunks,)),
     ]
     if tail:
-        out_shape = [jax.ShapeDtypeStruct(p_shape, f32), jax.ShapeDtypeStruct((blk_count,) + m_shape, f32)]
-        out_specs = [in_vmem, anywhere]
+        out_shape = [jax.ShapeDtypeStruct(p_shape, f32), jax.ShapeDtypeStruct((blk_count,) + m_shape, f32), picked]
+        out_specs = [in_vmem, anywhere, in_smem]
         flat_p, flat_m = (COARSE * share, 2 * wide), (2 * FINE * share, wide)
         scratch += [
             pltpu.VMEM((z_count,) + m_shape, f32),
@@ -312,11 +369,11 @@
             dma(()),
         ]
     else:
-        out_shape = [jax.ShapeDtypeStruct(plus_shape, f32), jax.ShapeDtypeStruct(minus_shape, f32)]
-        out_specs = [in_vmem, in_vmem]
+        out_shape = [jax.ShapeDtypeStruct(plus_shape, f32), jax.ShapeDtypeStruct(minus_shape, f32), picked]
+        out_specs = [in_vmem, in_vmem, in_smem]
     return pl.pallas_call(
         functools.partial(fused_kernel, chan, bound, tail),
-        in_specs=[anywhere] + [in_vmem] * 4,
+        in_specs=[anywhere, in_smem] + [in_vmem] * 5,
         out_specs=out_specs,
         out_shape=out_shape,
         scratch_shapes=scratch,
@@ -326,57 +383,20 @@
         cost_estimate=pl.CostEstimate(
             flops=8 * wide * wide * frequencies * 2, bytes_accessed=16 * wide * wide, transcendentals=0
         ),
-    )(rows, pack, unpack, by_chunk(cos), by_chunk(sin))
+    )(rows, pairing, fibre_lists, fibre_lists.T, places, by_chunk(cos), by_chunk(sin))
 
 
 def local(spectra, fibre_lists, pairing):
     seg_all, held, _, frequencies = spectra.shape
-    blk_count = lax.axis_size("blk")
-    seg_count = lax.axis_size("seg")
-    blk_index = lax.axis_index("blk")
-    block_count, chan = fibre_lists.shape
-    width = held * seg_count
+    blk_count, seg_count = lax.axis_size("blk"), lax.axis_size("seg")
+    chan = fibre_lists.shape[1]
     bound = 2 * (3 * chan // (2 * blk_count))
-    partner = pairing[0]
-
-    blocks = jnp.arange(block_count, dtype=jnp.int32)
-    leads = assign(partner)
-    owner = jnp.where(leads, blocks, partner) // 2
-    lead_parity = (~leads[0::2]).astype(jnp.int32)
-    lead = 2 * jnp.arange(blk_count, dtype=jnp.int32) + lead_parity
-    follow = take_small(partner, lead)
-    i32 = jnp.int32
-
-    mine = blk_index * width + jnp.arange(width, dtype=i32)
-    flat = fibre_lists.reshape(-1)
-    flat_owner = jnp.repeat(owner, chan)
-    pair_of = jnp.sum(jnp.where(flat[:, None] == mine[None, :], flat_owner[:, None], 0), axis=0)
-    order = jnp.arange(width, dtype=i32)
-    rank = jnp.sum((pair_of[:, None] == pair_of[None, :]) & (order[:, None] < order[None, :]), axis=0).astype(i32)
-    spot = pair_of * bound + rank
-    hit = jnp.arange(blk_count * bound, dtype=i32)[:, None] == spot[None, :]
-    hit = hit.reshape(blk_count, 1, bound, seg_count, 1, held)
-    part = jnp.arange(2, dtype=i32)
-    same = (part[:, None] == part[None, :]).reshape(1, 2, 1, 1, 2, 1)
-    pack = (hit & same).astype(jnp.bfloat16).reshape(blk_count * 2 * bound, 2 * width)
-
-    pair = jnp.concatenate(
-        [jnp.take(fibre_lists, lead[blk_index], axis=0), jnp.take(fibre_lists, follow[blk_index], axis=0)]
-    )
-    source = pair // width
-    rank = jnp.sum((source[:, None] == source[None, :]) & (pair[None, :] < pair[:, None]), axis=1).astype(i32)
-    spot = source * bound + rank
-    hit = spot[:, None] == jnp.arange(blk_count * bound, dtype=i32)[None, :]
-    hit = hit.reshape(1, 2 * chan, blk_count, 1, bound)
-    same = (part[:, None] == part[None, :]).reshape(2, 1, 1, 2, 1)
-    unpack = (hit & same).astype(jnp.bfloat16).reshape(4 * chan, blk_count * 2 * bound)
 
     rows = jnp.transpose(spectra, (0, 2, 1, 3)).reshape(seg_all, 2 * held, frequencies)
     share = chan // seg_count
     tail = share % 8 == 0
-    plus, minus = correlate(rows, pack, unpack, chan, bound, tail)
-    lead_here = lead[blk_index]
-    came_from = take_small(owner, (lead_here ^ 1)[None])[0]
+    plus, minus, chosen = correlate(rows, pairing, fibre_lists, bound, tail)
+    came_from = chosen[0]
     scaling = 1.0 / math.sqrt(frequencies * seg_all)
     if tail:
         other = lax.dynamic_index_in_dim(minus, came_from, 0, keepdims=False)
@@ -389,7 +409,7 @@
     own = jnp.transpose(own, (1, 3, 0, 2)).reshape(share, chan, LH) * scaling
     got = other.reshape(2 * FINE, share, COARSE, chan)[::-1]
     got = jnp.transpose(got, (1, 3, 2, 0)).reshape(share, chan, LH) * scaling
-    first = lead_here % 2 == 0
+    first = chosen[1] == 0
     return jnp.stack([jnp.where(first, own, got), jnp.where(first, got, own)])[None]
 
 

time: 136 us -> 123 us (0.904)
  other arithmetic: 9 us -> 1.41 us
  between operations: 8.04 us -> 2.6 us
    reduce_sum x8 -> x0, other arithmetic: 3.27 us -> none  [the longest x5 2.78 us: take_small(): return jnp.sum(jnp.where(hit, table[None, :], 0), axis=1)]
    convert_element_type x3 -> x0, local copies, waits for them, and re-layouts: 2.03 us -> none  [the longest x2 1.19 us: local(): (hit & same).astype(jnp.bfloat16).reshape(blk_count * 2 * bound, 2 * width)]
    transpose x1, local copies, waits for them, and re-layouts: 2.66 us -> 4.22 us  [local(): jnp.transpose(spectra, (0, 2, 1, 3)).reshape(seg_all, 2 * held, frequencies)]
    select_n x3 -> x0, other arithmetic: 1.53 us -> none  [the longest x1 0.78 us: local(): jnp.take(fibre_lists, lead[blk_index], axis=0)]
where the time goes in v3:
time: 123 us; the launch traced here: 122 us
  Pallas kernels  109 us (89%)
  local copies, waits for them, and re-layouts  9.91 us (8%)
  between operations  2.6 us (2%)
  other arithmetic  1.41 us (1%)
    pallas_call x1, Pallas kernels, correlate(): pl.pallas_call(functools.partial(fused_kernel, chan, bound, tail), in_spe...  109 us
    transpose x1, local copies, waits for them, and re-layouts, local(): jnp.transpose(spectra, (0, 2, 1, 3)).reshape(seg_all, 2 * held, frequencies)  4.22 us

profile of v3, /device:TPU:25, one launch (start us, length us, event | category | flops | bytes accessed | tf_op | source)
XLA Modules:
  0.0 122.4 jit_solution(14939839327680065621)
XLA Ops:
  0.0 1.4 %copy.12 = s32[8,64]{0,1:T(8,128)} copy(s32[8,64]{1,0:T(8,128)} %lists.1) | data formatting | bytes 4096 | tf_op args[1]
  1.4 4.2 %copy.11 = bf16[8,2,16,4096]{3,2,1,0:T(8,128)(2,1)} copy(bf16[8,2,16,4096]{3,1,2,0:T(2,128)(2,1)} %bitcast.17) | data formatting | bytes 4194304 | tf_op jit(solution)/shard_map/transpose | solution.py:395
  5.6 108.5 %shard_map.64 = (f32[8,8,1024]{2,1,0:T(8,128)}, f32[4,16,8,512]{3,2,1,0:T(8,128)}, s32[2]{0:T(128)}) custom-call(bf16[8,32,4096]{2,1,0:T(8,128)(2,1)} %bitcast.18, s32[1,8]{1,0:T(1,128)} %pairing.1, s32[8,64]{1,0:T(8,128)} %lists.1, s32[64,8]{1,0:T(8,128)} %bitcast.21, s32[258,256]{1,0:T(8,128)} %constant.17.clone.places, ...), custom_call_target="tpu_custom_call" | custom-call | flops 17179869184 | bytes 4194304 | tf_op jit(solution)/shard_map/pallas_call | solution.py:374
  114.1 1.3 %fusion = (s32[1]{0:T(128)}, s32[1]{0:T(128)}) fusion(s32[2]{0:T(128)} %get-tuple-element.8), kind=kLoop, calls=%fused_computation.6 | loop fusion | bytes 16 | tf_op jit(solution)/shard_map/slice | solution.py:412
  118.0 1.0 constant_dynamic-slice_fusion
  119.0 0.1 reshape.61
  119.1 1.0 broadcast_multiply_fusion
  120.1 0.1 mul.40
  120.2 0.4 bitcast_select_fusion.1
  120.6 0.3 copy.14
  120.9 0.3 copy.15
  121.2 0.1 maximum_bitcast_fusion
  121.3 1.1 copy.16

commit v4 on v3

--- a/solution.py
+++ b/solution.py
@@ -13,7 +13,7 @@
 STEP = 16
 COARSE = LH // STEP
 FINE = STEP // 2
-CHUNK = 512
+CHUNK = 256
 NT = (((1,), (1,)), ((), ()))
 
 
@@ -25,8 +25,9 @@
     return np.cos(angles).astype(np.float32), np.sin(angles).astype(np.float32)
 
 
-def plan(chan, bound, width, blk, blk_count, pairing, lists, lists_t, places, pack, unpack, chosen):
+def plan(chan, bound, width, blk, blk_count, pairing, lists, places, pack, unpack):
     count = lists.shape[0]
+    lists_t = jnp.swapaxes(lists[...], 0, 1)
     i32, f32, bf = jnp.int32, jnp.float32, jnp.bfloat16
 
     def lowest(block):
@@ -48,8 +49,6 @@
         lead = jnp.where(blk == k, jnp.where(first, 2 * k, 2 * k + 1), lead)
         came_from = jnp.where(blk == k, jnp.where(first, owner[2 * k + 1], owner[2 * k]), came_from)
     follow = pairing[0, lead]
-    chosen[0] = came_from
-    chosen[1] = lead % 2
 
     columns = places.shape[1]
     number = places[0:1, :]
@@ -85,15 +84,20 @@
         for part in range(2):
             hit = lane == spot + part * bound
             unpack[(2 * part + r) * chan : (2 * part + r + 1) * chan, :] = jnp.where(hit, 1.0, 0.0).astype(bf)
+    return came_from, lead & 1
+
+
+def lag_order(blocks):
+    return jnp.swapaxes(jnp.swapaxes(jnp.stack(blocks), 0, 1), 1, 2)
 
 
 def fused_kernel(
-    chan, bound, tail, rows_ref, pairing, lists, lists_t, places, cos_ref, sin_ref, *rest
+    chan, bound, tail, scaling, rows_ref, pairing, lists, places, cos_ref, sin_ref, *rest
 ):
     if tail:
-        own_ref, others_ref, chosen, *rest = rest
+        out_ref, *rest = rest
     else:
-        plus_out, minus_out, chosen, *rest = rest
+        plus_out, minus_out, picks_out, *rest = rest
     pack, unpack, col, packed, arr, xp, xm, yp, plus, minus, a_send, a_recv, b_send, b_recv, local_sem, *rest = rest
     blk_count, seg_count = lax.axis_size("blk"), lax.axis_size("seg")
     blk, seg = lax.axis_index("blk"), lax.axis_index("seg")
@@ -156,7 +160,7 @@
 
     plus[...] = jnp.zeros_like(plus)
     minus[...] = jnp.zeros_like(minus)
-    plan(chan, bound, seg_count * held // 2, blk, blk_count, pairing, lists, lists_t, places, pack, unpack, chosen)
+    came_from, parity = plan(chan, bound, seg_count * held // 2, blk, blk_count, pairing, lists, places, pack, unpack)
 
     def route(k):
         for step in range(1, seg_count):
@@ -214,7 +218,7 @@
     work(chunks - 1)
 
     if tail:
-        from_core_m, from_core_p, stage_m, stage_p, from_z_m, from_z_p, done, c_send, c_recv, z_send, z_recv, o_send, o_recv, own_sem = rest
+        from_core_m, from_core_p, stage_m, stage_p, from_z_m, from_z_p, done, others_ref, c_send, c_recv, z_send, z_recv, o_send, o_recv, own_sem = rest
         share = chan // seg_count
         z_count = seg_count // 2
         core, z = lax.rem(seg, 2), lax.div(seg, 2)
@@ -285,10 +289,19 @@
         for step in range(1, blk_count):
             o_copy(step).start()
         keep.start()
-        own_ref[...] = finish(1)
+        total = finish(1)
+        own = lag_order(
+            [total[a, :, c * chan : (c + 1) * chan] for a in range(COARSE) for c in range(2 * FINE)]
+        ) * scaling
         keep.wait()
         for step in range(1, blk_count):
             o_copy(step).wait()
+        theirs = others_ref[came_from]
+        got = lag_order(
+            [theirs[c, :, a * chan : (a + 1) * chan] for a in range(COARSE) for c in reversed(range(2 * FINE))]
+        ) * scaling
+        out_ref[0] = jnp.where(parity == 0, own, got)
+        out_ref[1] = jnp.where(parity == 0, got, own)
         for side in range(2):
             for step in order:
                 c_copy(side, step).wait_send()
@@ -297,6 +310,8 @@
     else:
         plus_out[...] = plus[...]
         minus_out[...] = minus[...]
+        picks_out[0] = came_from
+        picks_out[1] = parity
 
     @pl.loop(0, chunks)
     def _(k):
@@ -306,7 +321,7 @@
             b_copy(k, step).wait_send()
 
 
-def correlate(rows, pairing, fibre_lists, bound, tail):
+def correlate(rows, pairing, fibre_lists, bound, tail, scaling):
     held, frequencies = rows.shape[1], rows.shape[2]
     chan = fibre_lists.shape[1]
     blk_count, seg_count = lax.axis_size("blk"), lax.axis_size("seg")
@@ -317,8 +332,8 @@
         return np.ascontiguousarray(table.reshape(-1, chunks, CHUNK).transpose(1, 0, 2))
 
     slots = np.arange(seg_count * held)
-    number = slots // held * (held // 2) + slots % (held // 2)
-    part = slots // (held // 2) % 2
+    number = slots // 2
+    part = slots % 2
     across = np.broadcast_to(number[:, None], (slots.size, slots.size))
     places = np.concatenate([number[None], part[None], across]).astype(np.int32)
 
@@ -349,8 +364,8 @@
         dma((chunks,)),
     ]
     if tail:
-        out_shape = [jax.ShapeDtypeStruct(p_shape, f32), jax.ShapeDtypeStruct((blk_count,) + m_shape, f32), picked]
-        out_specs = [in_vmem, anywhere, in_smem]
+        out_shape = [jax.ShapeDtypeStruct((2, share, chan, LH), f32)]
+        out_specs = [in_vmem]
         flat_p, flat_m = (COARSE * share, 2 * wide), (2 * FINE * share, wide)
         scratch += [
             pltpu.VMEM((z_count,) + m_shape, f32),
@@ -360,6 +375,7 @@
             pltpu.VMEM((z_count,) + flat_m, bf),
             pltpu.VMEM((z_count,) + flat_p, bf),
             pltpu.VMEM(m_shape, f32),
+            pltpu.VMEM((blk_count,) + m_shape, f32),
             dma((2, z_count)),
             dma((2, z_count)),
             dma((2, z_count)),
@@ -372,8 +388,8 @@
         out_shape = [jax.ShapeDtypeStruct(plus_shape, f32), jax.ShapeDtypeStruct(minus_shape, f32), picked]
         out_specs = [in_vmem, in_vmem, in_smem]
     return pl.pallas_call(
-        functools.partial(fused_kernel, chan, bound, tail),
-        in_specs=[anywhere, in_smem] + [in_vmem] * 5,
+        functools.partial(fused_kernel, chan, bound, tail, scaling),
+        in_specs=[anywhere, in_smem] + [in_vmem] * 4,
         out_specs=out_specs,
         out_shape=out_shape,
         scratch_shapes=scratch,
@@ -383,7 +399,7 @@
         cost_estimate=pl.CostEstimate(
             flops=8 * wide * wide * frequencies * 2, bytes_accessed=16 * wide * wide, transcendentals=0
         ),
-    )(rows, pairing, fibre_lists, fibre_lists.T, places, by_chunk(cos), by_chunk(sin))
+    )(rows, pairing, fibre_lists, places, by_chunk(cos), by_chunk(sin))
 
 
 def local(spectra, fibre_lists, pairing):
@@ -392,19 +408,18 @@
     chan = fibre_lists.shape[1]
     bound = 2 * (3 * chan // (2 * blk_count))
 
-    rows = jnp.transpose(spectra, (0, 2, 1, 3)).reshape(seg_all, 2 * held, frequencies)
+    rows = spectra.reshape(seg_all, 2 * held, frequencies)
     share = chan // seg_count
     tail = share % 8 == 0
-    plus, minus, chosen = correlate(rows, pairing, fibre_lists, bound, tail)
-    came_from = chosen[0]
     scaling = 1.0 / math.sqrt(frequencies * seg_all)
+    results = correlate(rows, pairing, fibre_lists, bound, tail, scaling)
     if tail:
-        other = lax.dynamic_index_in_dim(minus, came_from, 0, keepdims=False)
-    else:
-        plus = lax.psum_scatter(plus, "seg", scatter_dimension=1, tiled=True)
-        other = lax.psum_scatter(minus, "seg", scatter_dimension=1, tiled=True)
-        others = lax.all_gather(other, "blk", axis=0)
-        other = lax.dynamic_index_in_dim(others, came_from, 0, keepdims=False)
+        return results[0][None]
+    plus, minus, chosen = results
+    plus = lax.psum_scatter(plus, "seg", scatter_dimension=1, tiled=True)
+    minus = lax.psum_scatter(minus, "seg", scatter_dimension=1, tiled=True)
+    others = lax.all_gather(minus, "blk", axis=0)
+    other = lax.dynamic_index_in_dim(others, chosen[0], 0, keepdims=False)
     own = plus.reshape(COARSE, share, 2 * FINE, chan)
     own = jnp.transpose(own, (1, 3, 0, 2)).reshape(share, chan, LH) * scaling
     got = other.reshape(2 * FINE, share, COARSE, chan)[::-1]

time: 123 us -> 118 us (0.959)
  local copies, waits for them, and re-layouts: 9.91 us -> 6 us
  Pallas kernels: 109 us -> 112 us
  between operations: 2.6 us -> 0.01 us
  other arithmetic: 1.41 us -> 0 us
    transpose x1 -> x0, local copies, waits for them, and re-layouts: 4.22 us -> none  [local(): jnp.transpose(spectra, (0, 2, 1, 3)).reshape(seg_all, 2 * held, frequencies)]
    reshape x1, local copies, waits for them, and re-layouts: 0.14 us -> 4.11 us  [local(): rows = spectra.reshape(seg_all, 2 * held, frequencies)]
    pallas_call x1, Pallas kernels: 109 us -> 112 us  [correlate(): pl.pallas_call(functools.partial(fused_kernel, chan, bound, tail, scaling...]
    slice x1 -> x0, local copies, waits for them, and re-layouts: 1.33 us -> none  [local(): first = chosen[1] == 0]
where the time goes in v4:
time: 118 us
  Pallas kernels  112 us (95%)
  local copies, waits for them, and re-layouts  6 us (5%)
    pallas_call x1, Pallas kernels, correlate(): pl.pallas_call(functools.partial(fused_kernel, chan, bound, tail, scaling...  112 us
    reshape x1, local copies, waits for them, and re-layouts, local(): rows = spectra.reshape(seg_all, 2 * held, frequencies)  4.11 us

profile of v4, /device:TPU:25, one launch (start us, length us, event | category | flops | bytes accessed | tf_op | source)
XLA Modules:
  0.0 118.1 jit_solution(259375153991148026)
XLA Ops:
  0.0 4.1 %reshape.3.rows_ref = bf16[8,32,4096]{2,1,0:T(8,128)(2,1)} reshape(bf16[8,16,2,4096]{3,2,1,0:T(2,128)(2,1)} %param.6) | data formatting | bytes 4194304 | tf_op jit(solution)/shard_map/reshape | solution.py:411
  4.1 112.1 %shard_map.64 = f32[2,8,64,128]{3,2,1,0:T(8,128)} custom-call(bf16[8,32,4096]{2,1,0:T(8,128)(2,1)} %reshape.3.rows_ref, s32[1,8]{1,0:T(1,128)} %pairing.1, s32[8,64]{1,0:T(8,128)} %lists.1, s32[258,256]{1,0:T(8,128)} %constant.6.clone.places, f32[16,16,256]{2,1,0:T(8,128)} %constant.7.clone.cos_ref, f32[16,16,256]{2,1,0:T(8,128)} %constant.8.clone.sin_ref), custom_call_target="tpu_custom_call" | custom-call | flops 17179869184 | bytes 4194304 | tf_op jit(solution)/shard_map/pallas_call | solution.py:390
  116.2 1.9 %copy.8 = f32[1,2,8,64,128]{4,3,2,1,0:T(8,128)} copy(f32[1,2,8,64,128]{4,3,2,1,0:T(8,128)} %bitcast.1) | data formatting | bytes 1048576

commit v5 on v4

--- a/solution.py
+++ b/solution.py
@@ -13,7 +13,8 @@
 STEP = 16
 COARSE = LH // STEP
 FINE = STEP // 2
-CHUNK = 256
+CHUNK = 512
+AHEAD = 3
 NT = (((1,), (1,)), ((), ()))
 
 
@@ -152,11 +153,13 @@
     def b_own(k):
         return pltpu.make_async_copy(packed.at[k, blk], arr.at[k, blk], b_send.at[k, 0])
 
-    @pl.loop(0, chunks)
-    def _(k):
+    def launch(k):
         for step in range(1, seg_count):
             a_copy(k, step).start()
         a_own(k).start()
+
+    ahead = min(AHEAD, chunks)
+    pl.loop(0, ahead)(launch)
 
     plus[...] = jnp.zeros_like(plus)
     minus[...] = jnp.zeros_like(minus)
@@ -199,19 +202,31 @@
             yp[back, im] = (ic + rs).astype(bf)
         tile = 4 * chan
 
+        @pl.loop(0, xm.shape[0] // tile)
+        def _(t):
+            at = pl.ds(pl.multiple_of(t * tile, tile), tile)
+            term = lax.dot_general(yp[...], xm[at, :], NT, preferred_element_type=jnp.float32)
+            minus[:, :, at] += term.reshape(2 * FINE, chan, tile)
+
         @pl.loop(0, yp.shape[0] // tile)
         def _(t):
             at = pl.ds(pl.multiple_of(t * tile, tile), tile)
-            y = yp[at, :]
-            first = lax.dot_general(xp[...], y, NT, preferred_element_type=jnp.float32)
-            plus[:, :, at] += first.reshape(COARSE, chan, tile)
-            second = lax.dot_general(y, xm[...], NT, preferred_element_type=jnp.float32)
-            minus[pl.ds(t * 4, 4)] += second.reshape(4, chan, COARSE * chan)
+            term = lax.dot_general(xp[...], yp[at, :], NT, preferred_element_type=jnp.float32)
+            plus[:, :, at] += term.reshape(COARSE, chan, tile)
+
+    def a_sent(k):
+        for step in range(1, seg_count):
+            a_copy(k, step).wait_send()
 
     route(0)
 
     @pl.loop(1, chunks)
     def _(k):
+        @pl.when(k + ahead - 1 < chunks)
+        def _():
+            a_sent(k - 1)
+            launch(k + ahead - 1)
+
         route(k)
         work(k - 1)
 
@@ -289,10 +304,6 @@
         for step in range(1, blk_count):
             o_copy(step).start()
         keep.start()
-        total = finish(1)
-        own = lag_order(
-            [total[a, :, c * chan : (c + 1) * chan] for a in range(COARSE) for c in range(2 * FINE)]
-        ) * scaling
         keep.wait()
         for step in range(1, blk_count):
             o_copy(step).wait()
@@ -300,6 +311,12 @@
         got = lag_order(
             [theirs[c, :, a * chan : (a + 1) * chan] for a in range(COARSE) for c in reversed(range(2 * FINE))]
         ) * scaling
+        out_ref[0] = got
+        total = finish(1)
+        own = lag_order(
+            [total[a, :, c * chan : (c + 1) * chan] for a in range(COARSE) for c in range(2 * FINE)]
+        ) * scaling
+        got = out_ref[0]
         out_ref[0] = jnp.where(parity == 0, own, got)
         out_ref[1] = jnp.where(parity == 0, got, own)
         for side in range(2):
@@ -313,10 +330,10 @@
         picks_out[0] = came_from
         picks_out[1] = parity
 
+    pl.loop(chunks - ahead, chunks)(a_sent)
+
     @pl.loop(0, chunks)
     def _(k):
-        for step in range(1, seg_count):
-            a_copy(k, step).wait_send()
         for step in range(1, blk_count):
             b_copy(k, step).wait_send()
 

time: 118 us -> 111 us (0.941)
  Pallas kernels: 112 us -> 104 us
    pallas_call x1, Pallas kernels: 112 us -> 104 us  [correlate(): pl.pallas_call(functools.partial(fused_kernel, chan, bound, tail, scaling...]
where the time goes in v5:
time: 111 us; the launch traced here: 110 us
  Pallas kernels  104 us (94%)
  local copies, waits for them, and re-layouts  6 us (5%)
    pallas_call x1, Pallas kernels, correlate(): pl.pallas_call(functools.partial(fused_kernel, chan, bound, tail, scaling...  104 us
    reshape x1, local copies, waits for them, and re-layouts, local(): rows = spectra.reshape(seg_all, 2 * held, frequencies)  4.11 us

profile of v5, /device:TPU:25, one launch (start us, length us, event | category | flops | bytes accessed | tf_op | source)
XLA Modules:
  0.0 110.2 jit_solution(12735061446518657039)
XLA Ops:
  0.0 4.1 %reshape.3.rows_ref = bf16[8,32,4096]{2,1,0:T(8,128)(2,1)} reshape(bf16[8,16,2,4096]{3,2,1,0:T(2,128)(2,1)} %param.6) | data formatting | bytes 4194304 | tf_op jit(solution)/shard_map/reshape | solution.py:428
  4.1 104.2 %shard_map.64 = f32[2,8,64,128]{3,2,1,0:T(8,128)} custom-call(bf16[8,32,4096]{2,1,0:T(8,128)(2,1)} %reshape.3.rows_ref, s32[1,8]{1,0:T(1,128)} %pairing.1, s32[8,64]{1,0:T(8,128)} %lists.1, s32[258,256]{1,0:T(8,128)} %constant.6.clone.places, f32[8,16,512]{2,1,0:T(8,128)} %constant.7.clone.cos_ref, f32[8,16,512]{2,1,0:T(8,128)} %constant.8.clone.sin_ref), custom_call_target="tpu_custom_call" | custom-call | flops 17179869184 | bytes 4194304 | tf_op jit(solution)/shard_map/pallas_call | solution.py:407
  108.3 1.9 %copy.8 = f32[1,2,8,64,128]{4,3,2,1,0:T(8,128)} copy(f32[1,2,8,64,128]{4,3,2,1,0:T(8,128)} %bitcast.1) | data formatting | bytes 1048576

commit v6 on v5

--- a/solution.py
+++ b/solution.py
@@ -104,7 +104,7 @@
     blk, seg = lax.axis_index("blk"), lax.axis_index("seg")
     chunks = col.shape[0]
     held = rows_ref.shape[1]
-    width = col.shape[2]
+    width = col.shape[3]
     bf = jnp.bfloat16
     mesh_ids = pl.DeviceIdType.MESH
 
@@ -124,8 +124,8 @@
     def a_copy(k, step):
         to = seg_peer(step)
         return pltpu.make_async_remote_copy(
-            src_ref=rows_ref.at[to, :, pl.ds(pl.multiple_of(k * width, width), width)],
-            dst_ref=col.at[k, pl.ds(pl.multiple_of(seg * held, held), held), :],
+            src_ref=rows_ref.at[to, :, :, pl.ds(pl.multiple_of(k * width, width), width)],
+            dst_ref=col.at[k, pl.ds(pl.multiple_of(seg * held, held), held)],
             send_sem=a_send.at[k, step],
             recv_sem=a_recv.at[k, step],
             device_id=(blk, to),
@@ -134,8 +134,8 @@
 
     def a_own(k):
         return pltpu.make_async_copy(
-            rows_ref.at[seg, :, pl.ds(pl.multiple_of(k * width, width), width)],
-            col.at[k, pl.ds(pl.multiple_of(seg * held, held), held), :],
+            rows_ref.at[seg, :, :, pl.ds(pl.multiple_of(k * width, width), width)],
+            col.at[k, pl.ds(pl.multiple_of(seg * held, held), held)],
             local_sem.at[k],
         )
 
@@ -163,13 +163,13 @@
 
     plus[...] = jnp.zeros_like(plus)
     minus[...] = jnp.zeros_like(minus)
-    came_from, parity = plan(chan, bound, seg_count * held // 2, blk, blk_count, pairing, lists, places, pack, unpack)
+    came_from, parity = plan(chan, bound, seg_count * held, blk, blk_count, pairing, lists, places, pack, unpack)
 
     def route(k):
         for step in range(1, seg_count):
             a_copy(k, step).wait_recv()
         a_own(k).wait()
-        mixed = jnp.dot(pack[...], col[k], preferred_element_type=jnp.float32).astype(bf)
+        mixed = jnp.dot(pack[...], col[k].reshape(2 * seg_count * held, width), preferred_element_type=jnp.float32).astype(bf)
         packed[k] = mixed.reshape(blk_count, 2 * bound, width)
         for step in range(1, blk_count):
             b_copy(k, step).start()
@@ -339,7 +339,7 @@
 
 
 def correlate(rows, pairing, fibre_lists, bound, tail, scaling):
-    held, frequencies = rows.shape[1], rows.shape[2]
+    held, frequencies = rows.shape[1], rows.shape[3]
     chan = fibre_lists.shape[1]
     blk_count, seg_count = lax.axis_size("blk"), lax.axis_size("seg")
     chunks = frequencies // CHUNK
@@ -348,7 +348,7 @@
     def by_chunk(table):
         return np.ascontiguousarray(table.reshape(-1, chunks, CHUNK).transpose(1, 0, 2))
 
-    slots = np.arange(seg_count * held)
+    slots = np.arange(2 * seg_count * held)
     number = slots // 2
     part = slots % 2
     across = np.broadcast_to(number[:, None], (slots.size, slots.size))
@@ -364,9 +364,9 @@
     in_vmem, anywhere = pl.BlockSpec(memory_space=pltpu.VMEM), pl.BlockSpec(memory_space=pl.ANY)
     in_smem, picked = pl.BlockSpec(memory_space=pltpu.SMEM), jax.ShapeDtypeStruct((2,), jnp.int32)
     scratch = [
-        pltpu.VMEM((blk_count * 2 * bound, seg_count * held), bf),
+        pltpu.VMEM((blk_count * 2 * bound, 2 * seg_count * held), bf),
         pltpu.VMEM((4 * chan, blk_count * 2 * bound), bf),
-        pltpu.VMEM((chunks, seg_count * held, CHUNK), bf),
+        pltpu.VMEM((chunks, seg_count * held, 2, CHUNK), bf),
         pltpu.VMEM((chunks, blk_count, 2 * bound, CHUNK), bf),
         pltpu.VMEM((chunks, blk_count, 2 * bound, CHUNK), bf),
         pltpu.VMEM((wide, 2 * CHUNK), bf),
@@ -420,16 +420,15 @@
 
 
 def local(spectra, fibre_lists, pairing):
-    seg_all, held, _, frequencies = spectra.shape
+    seg_all, frequencies = spectra.shape[0], spectra.shape[3]
     blk_count, seg_count = lax.axis_size("blk"), lax.axis_size("seg")
     chan = fibre_lists.shape[1]
     bound = 2 * (3 * chan // (2 * blk_count))
 
-    rows = spectra.reshape(seg_all, 2 * held, frequencies)
     share = chan // seg_count
     tail = share % 8 == 0
     scaling = 1.0 / math.sqrt(frequencies * seg_all)
-    results = correlate(rows, pairing, fibre_lists, bound, tail, scaling)
+    results = correlate(spectra, pairing, fibre_lists, bound, tail, scaling)
     if tail:
         return results[0][None]
     plus, minus, chosen = results

time: 111 us -> 106 us (0.955)
  local copies, waits for them, and re-layouts: 6 us -> 1.89 us
    reshape x1 -> x0, local copies, waits for them, and re-layouts: 4.11 us -> none  [local(): rows = spectra.reshape(seg_all, 2 * held, frequencies)]
where the time goes in v6:
time: 106 us
  Pallas kernels  104 us (98%)
  local copies, waits for them, and re-layouts  1.89 us (2%)
    pallas_call x1, Pallas kernels, correlate(): pl.pallas_call(functools.partial(fused_kernel, chan, bound, tail, scaling...  104 us

profile of v6, /device:TPU:25, one launch (start us, length us, event | category | flops | bytes accessed | tf_op | source)
XLA Modules:
  0.0 106.0 jit_solution(14721157487069827183)
XLA Ops:
  0.0 104.2 %shard_map.64 = f32[2,8,64,128]{3,2,1,0:T(8,128)} custom-call(bf16[8,16,2,4096]{3,2,1,0:T(2,128)(2,1)} %rows_ref.1, s32[1,8]{1,0:T(1,128)} %pairing.1, s32[8,64]{1,0:T(8,128)} %lists.1, s32[258,256]{1,0:T(8,128)} %constant.6.clone.places, f32[8,16,512]{2,1,0:T(8,128)} %constant.7.clone.cos_ref, f32[8,16,512]{2,1,0:T(8,128)} %constant.8.clone.sin_ref), custom_call_target="tpu_custom_call" | custom-call | flops 17179869184 | bytes 4194304 | tf_op jit(solution)/shard_map/pallas_call | solution.py:407
  104.2 1.9 %copy.8 = f32[1,2,8,64,128]{4,3,2,1,0:T(8,128)} copy(f32[1,2,8,64,128]{4,3,2,1,0:T(8,128)} %bitcast.1) | data formatting | bytes 1048576

commit v7 on v6

--- a/solution.py
+++ b/solution.py
@@ -175,7 +175,7 @@
             b_copy(k, step).start()
         b_own(k).start()
 
-    def work(k):
+    def work(k, minus_done=None):
         for step in range(1, blk_count):
             b_copy(k, step).wait_recv()
         b_own(k).wait()
@@ -208,6 +208,9 @@
             term = lax.dot_general(yp[...], xm[at, :], NT, preferred_element_type=jnp.float32)
             minus[:, :, at] += term.reshape(2 * FINE, chan, tile)
 
+        if minus_done:
+            minus_done()
+
         @pl.loop(0, yp.shape[0] // tile)
         def _(t):
             at = pl.ds(pl.multiple_of(t * tile, tile), tile)
@@ -230,10 +233,8 @@
         route(k)
         work(k - 1)
 
-    work(chunks - 1)
-
     if tail:
-        from_core_m, from_core_p, stage_m, stage_p, from_z_m, from_z_p, done, others_ref, c_send, c_recv, z_send, z_recv, o_send, o_recv, own_sem = rest
+        from_core_m, from_core_p, stage_m, stage_p, from_z_m, from_z_p, done, done_p, others_ref, c_send, c_recv, z_send, z_recv, o_send, o_recv, own_sem = rest
         share = chan // seg_count
         z_count = seg_count // 2
         core, z = lax.rem(seg, 2), lax.div(seg, 2)
@@ -257,37 +258,87 @@
                 device_id_type=mesh_ids,
             )
 
-        def z_copy(side, step):
+        def z_copy(side, step, to_z, slot):
             _, _, stage, landing = sides[side]
             return pltpu.make_async_remote_copy(
                 src_ref=stage.at[step],
-                dst_ref=landing.at[step],
+                dst_ref=landing.at[slot],
                 send_sem=z_send.at[side, step],
-                recv_sem=z_recv.at[side, step],
-                device_id=(blk, 2 * z_peer(step) + core),
+                recv_sem=z_recv.at[side, slot],
+                device_id=(blk, 2 * to_z + core),
                 device_id_type=mesh_ids,
             )
 
+        def z_direct(side, step):
+            return z_copy(side, step, z_peer(step), step)
+
+        def chip_terms(side, step):
+            acc, landing, _, _ = sides[side]
+            c_copy(side, step).wait_recv()
+            return acc[:, rows_of(2 * z_peer(step) + core), :] + landing[step]
+
+        def fill(side, step, value):
+            sides[side][2][step] = value.reshape(-1, value.shape[-1]).astype(bf)
+
+        def add_from(side, total, slot):
+            z_direct(side, slot).wait_recv()
+            return total + sides[side][3][slot].astype(jnp.float32).reshape(total.shape)
+
         order = list(range(1, z_count)) + [0]
+        relayed = z_count == 4
+        inward = jnp.where(z < 2, 1, 3)
+        outward = 4 - inward
+        is_end = (z == 0) | (z == 3)
+        last = chunks - 1
+
+        def minus_done():
+            for step in order:
+                c_copy(0, step).start()
+
+        work(last, minus_done)
+        for step in order:
+            c_copy(1, step).start()
+
         for side in range(2):
-            for step in order:
-                c_copy(side, step).start()
-        for side in range(2):
-            acc, landing, stage, _ = sides[side]
-            for step in order[:-1]:
-                c_copy(side, step).wait_recv()
-                both = acc[:, rows_of(2 * z_peer(step) + core), :] + landing[step]
-                stage[step] = both.reshape(-1, both.shape[-1]).astype(bf)
-                z_copy(side, step).start()
-
-        def finish(side):
-            acc, landing, _, terms = sides[side]
+            if relayed:
+                @pl.when(is_end)
+                def _():
+                    fill(side, outward, chip_terms(side, outward))
+                    z_copy(side, outward, z_peer(inward), 0).start()
+                    for step in (2, inward):
+                        fill(side, step, chip_terms(side, step))
+                        z_direct(side, step).start()
+
+                @pl.when(jnp.logical_not(is_end))
+                def _():
+                    fill(side, inward, chip_terms(side, inward))
+                    z_direct(side, inward).start()
+                    far = chip_terms(side, 2)
+                    fill(side, 2, add_from(side, far, 0))
+                    z_direct(side, 2).start()
+                    fill(side, outward, chip_terms(side, outward))
+                    z_direct(side, outward).start()
+            else:
+                for step in order[:-1]:
+                    fill(side, step, chip_terms(side, step))
+                    z_direct(side, step).start()
+
+        def finish(side, into):
+            acc, landing, _, _ = sides[side]
             c_copy(side, 0).wait_recv()
             total = acc[:, rows_of(seg), :] + landing[0]
-            for step in range(1, z_count):
-                z_copy(side, step).wait_recv()
-                total = total + terms[step].astype(jnp.float32).reshape(total.shape)
-            return total
+            if relayed:
+                total = add_from(side, total, outward)
+                total = add_from(side, total, 2)
+                into[...] = total
+
+                @pl.when(jnp.logical_not(is_end))
+                def _():
+                    into[...] = add_from(side, into[...], inward)
+            else:
+                for step in range(1, z_count):
+                    total = add_from(side, total, step)
+                into[...] = total
 
         def o_copy(step):
             return pltpu.make_async_remote_copy(
@@ -300,7 +351,7 @@
             )
 
         keep = pltpu.make_async_copy(done, others_ref.at[blk], own_sem)
-        done[...] = finish(0)
+        finish(0, done)
         for step in range(1, blk_count):
             o_copy(step).start()
         keep.start()
@@ -312,7 +363,8 @@
             [theirs[c, :, a * chan : (a + 1) * chan] for a in range(COARSE) for c in reversed(range(2 * FINE))]
         ) * scaling
         out_ref[0] = got
-        total = finish(1)
+        finish(1, done_p)
+        total = done_p[...]
         own = lag_order(
             [total[a, :, c * chan : (c + 1) * chan] for a in range(COARSE) for c in range(2 * FINE)]
         ) * scaling
@@ -323,8 +375,9 @@
             for step in order:
                 c_copy(side, step).wait_send()
             for step in order[:-1]:
-                z_copy(side, step).wait_send()
+                z_direct(side, step).wait_send()
     else:
+        work(chunks - 1)
         plus_out[...] = plus[...]
         minus_out[...] = minus[...]
         picks_out[0] = came_from
@@ -392,6 +445,7 @@
             pltpu.VMEM((z_count,) + flat_m, bf),
             pltpu.VMEM((z_count,) + flat_p, bf),
             pltpu.VMEM(m_shape, f32),
+            pltpu.VMEM(p_shape, f32),
             pltpu.VMEM((blk_count,) + m_shape, f32),
             dma((2, z_count)),
             dma((2, z_count)),

time: 106 us -> 98 us (0.925)
  the two profiles are of different devices: /device:TPU:25 before, /device:TPU:8 now
where the time goes in v7:
time: 98 us; the launch traced here: 97.8 us
  Pallas kernels  95.9 us (98%)
  local copies, waits for them, and re-layouts  1.89 us (2%)
    pallas_call x1, Pallas kernels, correlate(): pl.pallas_call(functools.partial(fused_kernel, chan, bound, tail, scaling...  95.9 us

profile of v7, /device:TPU:8, one launch (start us, length us, event | category | flops | bytes accessed | tf_op | source)
XLA Modules:
  0.0 97.8 jit_solution(1278548061691968176)
XLA Ops:
  0.0 95.9 %shard_map.64 = f32[2,8,64,128]{3,2,1,0:T(8,128)} custom-call(bf16[8,16,2,4096]{3,2,1,0:T(2,128)(2,1)} %rows_ref.1, s32[1,8]{1,0:T(1,128)} %pairing.1, s32[8,64]{1,0:T(8,128)} %lists.1, s32[258,256]{1,0:T(8,128)} %constant.6.clone.places, f32[8,16,512]{2,1,0:T(8,128)} %constant.7.clone.cos_ref, f32[8,16,512]{2,1,0:T(8,128)} %constant.8.clone.sin_ref), custom_call_target="tpu_custom_call" | custom-call | flops 17179869184 | bytes 4194304 | tf_op jit(solution)/shard_map/pallas_call | solution.py:461
  96.0 1.9 %copy.8 = f32[1,2,8,64,128]{4,3,2,1,0:T(8,128)} copy(f32[1,2,8,64,128]{4,3,2,1,0:T(8,128)} %bitcast.1) | data formatting | bytes 1048576

commit v8 on v7

--- a/solution.py
+++ b/solution.py
@@ -13,8 +13,8 @@
 STEP = 16
 COARSE = LH // STEP
 FINE = STEP // 2
-CHUNK = 512
-AHEAD = 3
+CHUNK = 256
+AHEAD = 6
 NT = (((1,), (1,)), ((), ()))
 
 
@@ -202,7 +202,7 @@
             yp[back, im] = (ic + rs).astype(bf)
         tile = 4 * chan
 
-        @pl.loop(0, xm.shape[0] // tile)
+        @pl.loop(0, xm.shape[0] // tile, unroll=2)
         def _(t):
             at = pl.ds(pl.multiple_of(t * tile, tile), tile)
             term = lax.dot_general(yp[...], xm[at, :], NT, preferred_element_type=jnp.float32)
@@ -211,7 +211,7 @@
         if minus_done:
             minus_done()
 
-        @pl.loop(0, yp.shape[0] // tile)
+        @pl.loop(0, yp.shape[0] // tile, unroll=2)
         def _(t):
             at = pl.ds(pl.multiple_of(t * tile, tile), tile)
             term = lax.dot_general(xp[...], yp[at, :], NT, preferred_element_type=jnp.float32)

time: 98 us -> 105 us (1.071)
  the two profiles are of different devices: /device:TPU:8 before, /device:TPU:0 now
where the time goes in v8:
time: 105 us
  Pallas kernels  103 us (98%)
  local copies, waits for them, and re-layouts  1.89 us (2%)
    pallas_call x1, Pallas kernels, correlate(): pl.pallas_call(functools.partial(fused_kernel, chan, bound, tail, scaling...  103 us

profile of v8, /device:TPU:0, one launch (start us, length us, event | category | flops | bytes accessed | tf_op | source)
XLA Modules:
  0.0 104.9 jit_solution(11885998068103636163)
XLA Ops:
  0.0 103.0 %shard_map.64 = f32[2,8,64,128]{3,2,1,0:T(8,128)} custom-call(bf16[8,16,2,4096]{3,2,1,0:T(2,128)(2,1)} %rows_ref.1, s32[1,8]{1,0:T(1,128)} %pairing.1, s32[8,64]{1,0:T(8,128)} %lists.1, s32[258,256]{1,0:T(8,128)} %constant.6.clone.places, f32[16,16,256]{2,1,0:T(8,128)} %constant.7.clone.cos_ref, f32[16,16,256]{2,1,0:T(8,128)} %constant.8.clone.sin_ref), custom_call_target="tpu_custom_call" | custom-call | flops 17179869184 | bytes 4194304 | tf_op jit(solution)/shard_map/pallas_call | solution.py:461
  103.0 1.9 %copy.8 = f32[1,2,8,64,128]{4,3,2,1,0:T(8,128)} copy(f32[1,2,8,64,128]{4,3,2,1,0:T(8,128)} %bitcast.1) | data formatting | bytes 1048576
